TPU v7x, 32 devices: a whole 2x2x4 slice. The times are simulated.
32 devices in a mesh: sec: 4 (over y, x), lat: 4 (over z), col: 2 (over core).
Axes of the slice: x: 2, y: 2, z: 4, core: 2. Of those that a mesh axis runs over, the one named last changes fastest.
Arguments:
- physical_state: bfloat16 [32, 64, 5120], P(('sec', 'lat', 'col')), may hold values from -6 to 6
- parallel_lengths: int32 [32], P(('sec', 'lat', 'col')), may hold values from 20 to 5120, as said below
- zonal_mode_assignment: int32 [856], replicated, may hold values from 0 to 640, as said below
- weighted_associated_polynomials: bfloat16 [856, 640, 32], P('lat', None, ('sec', 'col')), may hold values from -1 to 1
- marine_tracer_state: float32 [8, 128, 4096], P(None, ('sec', 'lat', 'col')), may hold values from -6 to 6
- lateral_diffusivity: float32 [128, 4096], P(('sec', 'lat', 'col')), may hold values from 0.015 to 0.15
- depthwise_diffusivity: float32 [128, 4096], P(('sec', 'lat', 'col')), may hold values from 0.02 to 0.2
- water_indicator: int32 [128, 4096], P(('sec', 'lat', 'col')), may hold values 0 or 1
- overlying_parallel: int32 [128], P(('sec', 'lat', 'col')), may hold values from 0 to 31, as said below
- underlying_marine_parallel: int32 [32], P(('sec', 'lat', 'col')), may hold values from 0 to 127, as said below
Outputs:
- harmonic_amounts: float32 [640, 856, 128], P(('sec', 'col'), 'lat')
- ocean_next: float32 [8, 128, 4096], P(None, ('sec', 'lat', 'col'))
Inputs may be any that keep to these rules, and one draw needn't show every extreme that they name: `parallel_lengths`: row j holds 20 + 4 * min(max(b + s * j, 0), 1275) points, with s = 42 and one offset b from (5100) // 4 - s * (31) to 0; the first row holds 20 points and the last 5120. `zonal_mode_assignment`: every wavenumber below 640 sits in exactly one slot; the other slots hold 640, meaning empty; slots s with equal s // 214 form a block, at least one block has all its slots taken. overlying_parallel[r] lies between (r // 4 - 1) * 1 and (r // 4 + 2) - 1; some rows reach the lower end and some the upper end. underlying_marine_parallel[j] lies between (j - 1) * 4 and (j + 2) * 4 - 1; some rows reach the lower end and some the upper end.
All inputs are finite; a program needn't handle non-finite values. No bound on the sum of `water_indicator` on one device may be relied on, other than what follows from the above.
Results may differ from a plain program's by a relative error of at most 0.004.
Values may be sent and summed in bfloat16 or wider, within the bound.
A program may use at most 256 MiB of HBM per device.

v0:
```python
import jax
import jax.numpy as jnp
from jax import lax
from jax.sharding import PartitionSpec as P

OSTEPS = 4


two_pi = 6.283185307179586
thermal_transfer_factor = 0.8
force_coef = 0.1


def extended(array, sides, width):
    for axis, dim in sides:
        count, length = (lax.axis_size(axis), array.shape[dim])
        up = [(i, (i + 1) % count) for i in range(count - 1)]
        down = [(j, i) for i, j in up]
        last = lax.slice_in_dim(array, length - width, length, axis=dim)
        initial = lax.slice_in_dim(array, 0, width, axis=dim)
        before = lax.ppermute(last, axis, up)
        after = lax.ppermute(initial, axis, down)
        array = jnp.concatenate([before, array, after], axis=dim)
    return array


def fourier_table(row_points, wave_count, grid_width):
    wave_index = jnp.arange(wave_count, dtype=jnp.int32)
    positions = jnp.arange(grid_width, dtype=jnp.int32)
    points_float = row_points.astype(jnp.float32)
    angle_unit = jnp.float32(two_pi) / points_float
    residue = wave_index[:, None] * positions[None, :] % row_points
    angle = residue.astype(jnp.float32) * angle_unit
    inside = (positions[None, :] < row_points) & (wave_index[:, None] < row_points // 2)
    norm_factor = 1.0 / jnp.sqrt(points_float)
    real_part = jnp.where(inside, jnp.cos(angle) * norm_factor, 0.0)
    imag_part = jnp.where(inside, -jnp.sin(angle) * norm_factor, 0.0)
    return jnp.stack([real_part, imag_part]).astype(jnp.bfloat16)


def advance_coupled_model(
    bordered_array,
    meridian_exchange_factor,
    zonal_exchange_factor,
    depthwise_exchange_factor,
    boundary_warming_term,
):
    centre = bordered_array[:, 1:-1]
    meridional = meridian_exchange_factor[1:] * (
        bordered_array[:, 2:] - centre
    ) - meridian_exchange_factor[:-1] * (centre - bordered_array[:, :-2])
    east_flux = zonal_exchange_factor * (jnp.roll(centre, -1, axis=2) - centre)
    zonal_div = east_flux - jnp.roll(east_flux, 1, axis=2)
    vertical_flux = depthwise_exchange_factor * (centre[1:] - centre[:-1])
    zero_layer = jnp.zeros_like(vertical_flux[:1])
    vertical = jnp.concatenate([vertical_flux, zero_layer], 0) - jnp.concatenate(
        [zero_layer, vertical_flux], 0
    )
    forced = jnp.concatenate([boundary_warming_term[None], jnp.zeros_like(centre[1:])], 0)
    return centre + meridional + zonal_div + vertical + forced


def face_coefs(sea_rows, kappa_rows):
    return 0.5 * (kappa_rows[:-1] + kappa_rows[1:]) * sea_rows[:-1] * sea_rows[1:]


def zonal_coefs(sea_rows, kappa_rows):
    return (
        0.5
        * (kappa_rows + jnp.roll(kappa_rows, -1, axis=1))
        * sea_rows
        * jnp.roll(sea_rows, -1, axis=1)
    )


def body(
    physical_state,
    parallel_lengths,
    zonal_mode_assignment,
    weighted_associated_polynomials,
    marine_tracer_state,
    lateral_diffusivity,
    depthwise_diffusivity,
    water_indicator,
    overlying_parallel,
    underlying_marine_parallel,
):
    sec_count = lax.axis_size("sec")
    lat_count = lax.axis_size("lat")
    col_count = lax.axis_size("col")
    rows_here = physical_state.shape[0]
    grid_width = physical_state.shape[2]
    strata_number = physical_state.shape[1] // 4
    vector_width = 2 * physical_state.shape[1]
    slot_count = weighted_associated_polynomials.shape[0]
    wave_count = weighted_associated_polynomials.shape[1]
    block_degrees = wave_count // (sec_count * col_count)

    def row_transform(row_pair):
        fourier_matrix = fourier_table(row_pair[1], wave_count, grid_width)
        result = jnp.einsum(
            "pmi,vi->mpv", fourier_matrix, row_pair[0], preferred_element_type=jnp.float32
        )
        return result.reshape(wave_count, vector_width).astype(jnp.bfloat16)

    fourier = lax.map(row_transform, (physical_state, parallel_lengths))
    outgoing = jnp.take(fourier, jnp.clip(zonal_mode_assignment, 0, wave_count - 1), axis=1)
    outgoing = outgoing.reshape(rows_here, lat_count, slot_count, vector_width)
    incoming = lax.all_to_all(outgoing, "lat", split_axis=1, concat_axis=0, tiled=True)
    incoming = incoming.reshape(lat_count * rows_here, slot_count, vector_width)
    own_waves = lax.dynamic_slice_in_dim(
        zonal_mode_assignment, lax.axis_index("lat") * slot_count, slot_count
    )
    group_index = lax.axis_index("sec") * col_count + lax.axis_index("col")
    degrees = group_index * block_degrees + jnp.arange(block_degrees, dtype=jnp.int32)
    harmonic_amounts = lax.psum_scatter(
        jnp.einsum(
            "snq,qsv->nsv",
            weighted_associated_polynomials,
            incoming,
            preferred_element_type=jnp.float32,
        ),
        ("sec", "col"),
        scatter_dimension=0,
        tiled=True,
    )
    harmonic_amounts = jnp.where(
        degrees[:, None, None] >= own_waves[None, :, None], harmonic_amounts, 0.0
    )
    linear_index = (
        lax.axis_index("sec") * lat_count + lax.axis_index("lat")
    ) * col_count + lax.axis_index("col")
    marine_parallel_entries = marine_tracer_state.shape[1]
    marine_span = marine_tracer_state.shape[2]
    water_share = water_indicator.astype(jnp.float32)
    topmost_layer = jnp.stack([marine_tracer_state[0], water_share, lateral_diffusivity])
    surface_padded = extended(topmost_layer, ((("sec", "lat", "col"), 1),), marine_parallel_entries)
    skin_warmth_parallels = jnp.take(
        surface_padded[0],
        underlying_marine_parallel - (linear_index - 1) * marine_parallel_entries,
        axis=0,
    )
    grid_points = jnp.arange(grid_width, dtype=jnp.int32)
    sea_column_index = jnp.minimum(
        grid_points[None, :] * marine_span // parallel_lengths[:, None], marine_span - 1
    )
    skin_warmth_mapped_upward = jnp.take_along_axis(skin_warmth_parallels, sea_column_index, axis=1)
    bottom_stratum = strata_number - 1
    zonal_wind = physical_state[:, bottom_stratum].astype(jnp.float32)
    meridional_wind = physical_state[:, strata_number + bottom_stratum].astype(jnp.float32)
    lowest_layer_warmth = physical_state[:, 2 * strata_number + bottom_stratum].astype(jnp.float32)
    breeze_speed = jnp.sqrt(zonal_wind * zonal_wind + meridional_wind * meridional_wind + 1.0)
    boundary_energy_exchange = (
        thermal_transfer_factor * breeze_speed * (skin_warmth_mapped_upward - lowest_layer_warmth)
    )
    ocean_points = jnp.arange(marine_span, dtype=jnp.int32)
    grid_column = ocean_points[None, :] * parallel_lengths[:, None] // marine_span
    flux_rows = jnp.take_along_axis(boundary_energy_exchange, grid_column, axis=1)
    flux_ext = extended(flux_rows, ((("sec", "lat", "col"), 0),), rows_here)
    forcing = jnp.take(flux_ext, overlying_parallel - (linear_index - 1) * rows_here, axis=0)
    depthwise_exchange_factor = depthwise_diffusivity * water_share
    boundary_warming_term = force_coef * water_share * forcing
    sea_ext = surface_padded[1, marine_parallel_entries - 1 : 2 * marine_parallel_entries + 1]
    kappa_ext = surface_padded[2, marine_parallel_entries - 1 : 2 * marine_parallel_entries + 1]
    meridian_exchange_factor = face_coefs(sea_ext, kappa_ext)
    zonal_exchange_factor = zonal_coefs(water_share, lateral_diffusivity)
    thermal_state = marine_tracer_state
    for iteration in range(OSTEPS):
        bordered_array = extended(thermal_state, ((("sec", "lat", "col"), 1),), 1)
        thermal_state = advance_coupled_model(
            bordered_array,
            meridian_exchange_factor,
            zonal_exchange_factor,
            depthwise_exchange_factor,
            boundary_warming_term,
        )
    return (harmonic_amounts, thermal_state)


def solution(mesh):
    return jax.shard_map(
        body,
        mesh=mesh,
        in_specs=(
            P(("sec", "lat", "col"), None, None),
            P(("sec", "lat", "col")),
            P(),
            P("lat", None, ("sec", "col")),
            P(None, ("sec", "lat", "col"), None),
            P(("sec", "lat", "col"), None),
            P(("sec", "lat", "col"), None),
            P(("sec", "lat", "col"), None),
            P(("sec", "lat", "col")),
            P(("sec", "lat", "col")),
        ),
        out_specs=(P(("sec", "col"), "lat", None), P(None, ("sec", "lat", "col"), None)),
        check_vma=False,
    )
```

profile of v0, /device:TPU:0, one launch (start us, length us, event | category | flops | bytes accessed | tf_op | source)
XLA Modules:
  0.0 728.0 jit_solution(4052868413350221279)
XLA Ops:
  9.5 177.4 %fusion = (bf16[1,640,5120]{2,1,0:T(8,128)(2,1)S(1)}, bf16[1,640,5120]{2,1,0:T(8,128)(2,1)S(1)}) fusion(f32[]{:T(128)S(6)} %sqrt.15, f32[]{:T(128)S(6)} %div.73, s32[]{:T(128)S(6)} %select_n.246, pred[]{:T(512)S(6)} %lt.136, pred[5120]{0:T(1024)(128)(4,1)S(1)} %iota_compare_fusion, pred[640]{0:T(1024)(128)(4,1)S(1)} %iota_compare_fusion.1), kind=kLoop, calls=%fused_computation.8 | loop fusion | flops 58982400 | bytes 13112973 | tf_op jit(solution)/shard_map/convert.1
  186.9 4.1 fusion.12
  191.2 2.4 gather_fusion
  193.9 14.1 %all_to_all.4 = bf16[1,4,214,128]{3,2,0,1:T(8,128)(2,1)S(1)} all-to-all(bf16[1,4,214,128]{3,2,0,1:T(8,128)(2,1)S(1)} %select_bitcast_fusion), channel_id=1, replica_groups=mesh['sec'=4,'lat'=4,'col'=2] {'lat'}, dimensions={1} | all-to-all | bytes 438272 | tf_op jit(solution)/shard_map/all_to_all | solution.py:109
  208.0 25.1 %convolution_bitcast_fusion = f32[640,214,128]{0,2,1:T(8,128)} fusion(bf16[214,640,4]{1,2,0:T(4,128)(2,1)S(1)} %copy-done, bf16[1,4,214,128]{3,2,0,1:T(8,128)(2,1)S(1)} %all_to_all.4), kind=kOutput, calls=%fused_computation.4 | convolution fusion | flops 140247040 | bytes 71438336 | tf_op jit(solution)/shard_map/snq,qsv->nsv/dot_general | solution.py:117
  233.1 69.5 %copy.21 = f32[640,214,128]{2,1,0:T(8,128)} copy(f32[640,214,128]{0,2,1:T(8,128)} %convolution_bitcast_fusion) | data formatting | bytes 140247040 | tf_op jit(solution)/shard_map/snq,qsv->nsv/transpose | solution.py:117
  303.7 1.3 collective-permute-start.1
  305.0 3.0 collective-permute-start
  309.0 1.9 collective-permute-start.3
  314.4 1.7 compare_select_fusion
  316.4 28.8 %gather_fusion.1 = f32[5120]{0:T(1024)S(1)} fusion(f32[4096]{0:T(1024)S(1)} %bitcast.58, s32[5120]{0:T(1024)S(1)} %broadcast_clamp_fusion), kind=kCustom, calls=%fused_computation.1 | custom fusion | bytes 61440 | tf_op jit(solution)/shard_map/jit(take_along_axis)/gather | solution.py:147
  345.2 2.9 bitcast_multiply_fusion
  348.1 23.0 %gather_fusion.2 = f32[4096]{0:T(1024)S(1)} fusion(f32[5120]{0:T(1024)S(1)} %bitcast.59, s32[4096]{0:T(1024)S(1)} %broadcast_clamp_fusion.1), kind=kCustom, calls=%fused_computation.2 | custom fusion | bytes 49152 | tf_op jit(solution)/shard_map/jit(take_along_axis)/gather | solution.py:158
  372.6 3.8 collective-permute-start.4
  379.8 3.7 collective-permute-start.7
  385.2 3.4 collective-permute-done.6
  390.0 5.5 collective-permute-start.9
  397.1 1.6 collective-permute-done.8
  400.2 5.0 collective-permute-start.11
  406.8 1.6 collective-permute-done.10
  408.4 1.6 pad_add_fusion
  410.0 295.9 %reduce-scatter.2.cloned.1.call-done = f32[80,214,128]{2,1,0:T(8,128)} async-done(((f32[640,214,128]{2,1,0:T(8,128)}), f32[80,214,128]{2,1,0:T(8,128)}) %reduce-scatter.2.cloned.1.call-update) | async-done | bytes 8765456 | tf_op jit(solution)/shard_map/reduce_scatter | solution.py:116
  705.9 10.0 %broadcast_select_fusion = f32[80,214,128]{2,1,0:T(8,128)S(1)} fusion(f32[80,214,128]{2,1,0:T(8,128)} %reduce-scatter.2.cloned.1.call-done, pred[80,214]{1,0:T(8,128)(4,1)S(1)} %broadcast_compare_fusion), kind=kLoop, calls=%fused_computation.21 | loop fusion | flops 2191360 | bytes 17548000 | tf_op jit(solution)/shard_map/jit(_where)/select_n | solution.py:127
  715.9 5.1 copy.22
  (91 shorter events, 19.5 us)
Async XLA Ops:
  7.2 200.9 %copy-start = (bf16[214,640,4]{1,2,0:T(4,128)(2,1)S(1)}, bf16[214,640,4]{1,2,0:T(4,128)(2,1)}, u32[]{:S(2)}) copy-start(bf16[214,640,4]{1,2,0:T(4,128)(2,1)} %param.13) | copy-start | bytes 3287044
  7.2 179.7 %copy-start.6 = (bf16[1,64,5120]{2,1,0:T(8,128)(2,1)S(1)}, bf16[1,64,5120]{2,1,0:T(8,128)(2,1)}, u32[]{:S(2)}) copy-start(bf16[1,64,5120]{2,1,0:T(8,128)(2,1)} %param.10) | copy-start | bytes 1966084
  7.2 698.7 %reduce-scatter.2.cloned.1.call-start = ((), (), s32[]{:S(2)}) async-start(), calls=%async_computation.2 | async-start | bytes 79626240 | tf_op jit(solution)/shard_map/reduce_scatter | solution.py:116
  302.6 1.0 copy-start.1
  302.6 1.0 copy-start.4
  302.6 1.1 copy-start.3
  302.6 11.7 %copy-start.7 = (s32[4]{0:T(128)S(1)}, s32[4]{0:T(128)}, u32[]{:S(2)}) copy-start(s32[4]{0:T(128)} %param.18) | copy-start | bytes 52
  303.7 12.5 %collective-permute-start.1 = (f32[3,4,4096]{2,1,0:T(4,128)S(1)}, f32[3,4,4096]{2,1,0:T(4,128)S(1)}, u32[]{:S(2)}, u32[]{:S(2)}) collective-permute-start(f32[3,4,4096]{2,1,0:T(4,128)S(1)} %pad_maximum_fusion.8), channel_id=1, source_target_pairs={{1,0},{2,1},{3,2},{4,3},{5,4},{6,5},{7,6},{8,7},{9,8},{10,9},{11,1... | collective-permute-start | bytes 589832 | tf_op jit(solution)/shard_map/ppermute | solution.py:22
  305.0 11.2 %collective-permute-start = (f32[3,4,4096]{2,1,0:T(4,128)S(1)}, f32[3,4,4096]{2,1,0:T(4,128)S(1)}, u32[]{:S(2)}, u32[]{:S(2)}) collective-permute-start(f32[3,4,4096]{2,1,0:T(4,128)S(1)} %pad_maximum_fusion.8), channel_id=1, source_target_pairs={{0,1},{1,2},{2,3},{3,4},{4,5},{5,6},{6,7},{7,8},{8,9},{9,10},{10,1... | collective-permute-start | bytes 589832 | tf_op jit(solution)/shard_map/ppermute | solution.py:21
  309.0 69.3 %collective-permute-start.3 = (f32[8,1,4096]{2,1,0:T(1,128)}, f32[8,1,4096]{2,1,0:T(1,128)S(1)}, u32[]{:S(2)}, u32[]{:S(2)}) collective-permute-start(f32[8,1,4096]{2,1,0:T(1,128)} %get-tuple-element.40), channel_id=1, source_target_pairs={{0,1},{1,2},{2,3},{3,4},{4,5},{5,6},{6,7},{7,8},{8,9},{9,10},{10,1... | collective-permute-start | bytes 393224 | tf_op jit(solution)/shard_map/ppermute | solution.py:21
  310.9 67.4 %collective-permute-start.2 = (f32[8,1,4096]{2,1,0:T(1,128)}, f32[8,1,4096]{2,1,0:T(1,128)S(1)}, u32[]{:S(2)}, u32[]{:S(2)}) collective-permute-start(f32[8,1,4096]{2,1,0:T(1,128)} %get-tuple-element.39), channel_id=1, source_target_pairs={{1,0},{2,1},{3,2},{4,3},{5,4},{6,5},{7,6},{8,7},{9,8},{10,9},{11,1... | collective-permute-start | bytes 393224 | tf_op jit(solution)/shard_map/ppermute | solution.py:22
  345.2 32.7 %copy-start.5 = (f32[4,4096]{1,0:T(4,128)S(1)}, f32[4,4096]{1,0:T(4,128)}, u32[]{:S(2)}) copy-start(f32[4,4096]{1,0:T(4,128)} %param.16) | copy-start | bytes 196612
  345.2 32.7 %copy-start.2 = (f32[8,4,4096]{2,1,0:T(4,128)S(1)}, f32[8,4,4096]{2,1,0:T(4,128)}, u32[]{:S(2)}) copy-start(f32[8,4,4096]{2,1,0:T(4,128)} %param.14) | copy-start | bytes 1572868
  345.2 32.7 %slice-start = ((f32[8,4,4096]{2,1,0:T(4,128)}), f32[8,4,1]{2,1,0:T(4,128)S(1)}, s32[]{:S(2)}) async-start(f32[8,4,4096]{2,1,0:T(4,128)} %param.14), calls=%async_computation.3 | async-start | bytes 32768 | tf_op jit(solution)/shard_map/jit(_roll_static)/slice | solution.py:52
  371.3 5.3 collective-permute-start.5
  372.6 4.6 collective-permute-start.4
  379.8 5.4 collective-permute-start.7
  383.5 5.0 collective-permute-start.6
  390.0 7.1 collective-permute-start.9
  395.5 3.2 collective-permute-start.8
  400.2 6.6 collective-permute-start.11
  405.2 3.2 collective-permute-start.10
Sparse Core Ops, SparseCore 0:
  302.7 403.1 reduce-scatter.1
where the time goes:
time: 743 us; the launch traced here: 728 us
  waiting for transfers between devices  303 us (41%)
  other arithmetic  200 us (27%)
  local copies, waits for them, and re-layouts  135 us (18%)
  starting transfers between devices  30.6 us (4%)
  matrix products  29.1 us (4%)
  between operations  16.4 us (2%)
  blocking collectives  14.1 us (2%)
    reduce_scatter x1, waiting for transfers between devices, body(): lax.psum_scatter(jnp.einsum('snq,qsv->nsv', weighted_associated_polynomia...  296 us
    another operation x1, other arithmetic  177 us
    transpose x1, local copies, waits for them, and re-layouts, body(): jnp.einsum('snq,qsv->nsv', weighted_associated_polynomials, incoming, pre...  69.5 us
    gather x1, local copies, waits for them, and re-layouts, body(): jnp.take_along_axis(skin_warmth_parallels, sea_column_index, axis=1)  28.8 us
    dot_general x1, matrix products, body(): jnp.einsum('snq,qsv->nsv', weighted_associated_polynomials, incoming, pre...  25.1 us
    gather x1, local copies, waits for them, and re-layouts, body(): jnp.take_along_axis(boundary_energy_exchange, grid_column, axis=1)  23 us
    ppermute x6, starting transfers between devices, extended(): before = lax.ppermute(last, axis, up)  22.8 us
  transfers between devices with their start and end apart: 13, of which 5 were waited for; matrix products, arithmetic and copies ran while one was open for 9% of the time, Pallas kernels for 0%

commit v1 on v0

v1 whole, which is shorter than its diff:
```python
import functools

import jax
import jax.numpy as jnp
from jax import lax
from jax.experimental import pallas as pl
from jax.experimental.pallas import tpu as pltpu
from jax.sharding import PartitionSpec as P

OSTEPS = 4
LOW = 8
CHUNK = 256
SLOT_PAD = 16

two_pi = 6.283185307179586
thermal_transfer_factor = 0.8
force_coef = 0.1

GROUP = ("sec", "col")
LINE = ("sec", "lat", "col")


def angle_tables(points, wave_count, grid_width):
    low = jnp.arange(LOW, dtype=jnp.float32)
    mid = jnp.arange(CHUNK // LOW, dtype=jnp.float32) * LOW
    high = jnp.arange(grid_width // CHUNK, dtype=jnp.float32) * CHUNK
    place = jnp.concatenate([low, mid, high])
    count = points.astype(jnp.float32)
    product = place[:, None] * jnp.arange(wave_count, dtype=jnp.float32)[None, :]
    residue = product - jnp.round(product / count) * count
    angle = residue * (jnp.float32(two_pi) / count)
    scale = jnp.where(jnp.arange(place.shape[0]) >= LOW + CHUNK // LOW, 1.0 / jnp.sqrt(count), 1.0)
    return jnp.stack([jnp.cos(angle), -jnp.sin(angle)]) * scale[None, :, None]


def fourier_kernel(points_ref, table_ref, slots_ref, x_ref, out_ref, base_ref, acc_ref):
    points = points_ref[0]
    waves = table_ref.shape[2]
    fields = x_ref.shape[0]
    chunks = x_ref.shape[1] // CHUNK
    low_c, low_s = table_ref[0, :LOW], table_ref[1, :LOW]
    for b in range(CHUNK // LOW):
        mid_c = table_ref[0, LOW + b : LOW + b + 1]
        mid_s = table_ref[1, LOW + b : LOW + b + 1]
        base_ref[0, b * LOW : (b + 1) * LOW] = low_c * mid_c - low_s * mid_s
        base_ref[1, b * LOW : (b + 1) * LOW] = low_c * mid_s + low_s * mid_c
    acc_ref[...] = jnp.zeros_like(acc_ref)
    top = LOW + CHUNK // LOW

    @pl.loop(0, chunks)
    def _(a):
        start = pl.multiple_of(a * CHUNK, CHUNK)
        position = start + lax.broadcasted_iota(jnp.int32, (fields, CHUNK), 1)
        block = x_ref[:, pl.ds(start, CHUNK)].astype(jnp.float32)
        block = jnp.where(position < points, block, 0.0).astype(jnp.bfloat16)
        high_c = table_ref[0, pl.ds(top + a, 1)]
        high_s = table_ref[1, pl.ds(top + a, 1)]
        for w in range(0, waves, 128):
            cut = slice(w, w + 128)
            base_c, base_s = base_ref[0, :, cut], base_ref[1, :, cut]
            turn_c, turn_s = high_c[:, cut], high_s[:, cut]
            real = (base_c * turn_c - base_s * turn_s).astype(jnp.bfloat16)
            imag = (base_c * turn_s + base_s * turn_c).astype(jnp.bfloat16)
            both = jnp.concatenate([real, imag], axis=1)
            part = jnp.dot(block, both, preferred_element_type=jnp.float32)
            acc_ref[:fields, cut] += part[:, :128]
            acc_ref[fields:, cut] += part[:, 128:]

    wave = lax.broadcasted_iota(jnp.int32, acc_ref.shape, 1)
    coefs = jnp.where(wave < points // 2, acc_ref[...], 0.0).astype(jnp.bfloat16)
    rows = 112 if slots_ref.shape[0] % 112 == 0 else slots_ref.shape[0] // 8

    @pl.loop(0, slots_ref.shape[0] // rows)
    def _(b):
        start = pl.multiple_of(b * rows, 16)
        held = slots_ref[pl.ds(start, rows)]
        pick = held == lax.broadcasted_iota(jnp.int32, (rows, waves), 1)
        pick = jnp.where(pick, 1.0, 0.0).astype(jnp.bfloat16)
        out_ref[pl.ds(start, rows)] = lax.dot_general(
            pick, coefs, (((1,), (1,)), ((), ())), preferred_element_type=jnp.float32
        ).astype(jnp.bfloat16)


def fourier_slots(state, points, slots):
    fields, width = state.shape
    waves = slots[1]
    table = angle_tables(points[0], waves, width)
    return pl.pallas_call(
        fourier_kernel,
        out_shape=jax.ShapeDtypeStruct((slots[0].shape[0], 2 * fields), jnp.bfloat16),
        in_specs=[
            pl.BlockSpec(memory_space=pltpu.SMEM),
            pl.BlockSpec(memory_space=pltpu.VMEM),
            pl.BlockSpec(memory_space=pltpu.VMEM),
            pl.BlockSpec(memory_space=pltpu.VMEM),
        ],
        out_specs=pl.BlockSpec(memory_space=pltpu.VMEM),
        scratch_shapes=[
            pltpu.VMEM((2, CHUNK, waves), jnp.float32),
            pltpu.VMEM((2 * fields, waves), jnp.float32),
        ],
        compiler_params=pltpu.CompilerParams(vmem_limit_bytes=32 * 2**20),
        cost_estimate=pl.CostEstimate(
            flops=4 * fields * waves * width, bytes_accessed=4 * 2**20, transcendentals=0
        ),
    )(points, table, slots[0], state)


def legendre_kernel(degree_ref, slots_ref, weight_ref, coef_ref, out_ref):
    rows, pair, width = coef_ref.shape
    degrees = out_ref.shape[1]
    first = degree_ref[0]
    for half in range(pair // 8):
        cut = slice(half * 8, half * 8 + 8)
        values = weight_ref[:, cut, :].astype(jnp.float32).reshape(rows * 8, weight_ref.shape[2])
        values = values.T[:degrees]
        lane_slot = lax.broadcasted_iota(jnp.int32, (degrees, rows * 8), 1) % 8
        coefs = coef_ref[:, cut, :].astype(jnp.float32).reshape(rows * 8, width).astype(jnp.bfloat16)
        degree = first + lax.broadcasted_iota(jnp.int32, (degrees, rows * 8), 0)
        for s in range(8):
            wave = slots_ref[pl.program_id(0) * pair + half * 8 + s]
            keep = (lane_slot == s) & (degree >= wave)
            left = jnp.where(keep, values, 0.0).astype(jnp.bfloat16)
            out_ref[half * 8 + s] = jnp.dot(left, coefs, preferred_element_type=jnp.float32)


def legendre(weights, coefs, slots, first_degree, slot_count, degrees):
    rows, padded, width = coefs.shape
    return pl.pallas_call(
        legendre_kernel,
        grid=(padded // SLOT_PAD,),
        out_shape=jax.ShapeDtypeStruct((slot_count, degrees, width), jnp.float32),
        in_specs=[
            pl.BlockSpec(memory_space=pltpu.SMEM),
            pl.BlockSpec(memory_space=pltpu.SMEM),
            pl.BlockSpec((rows, SLOT_PAD, weights.shape[2]), lambda i: (0, i, 0)),
            pl.BlockSpec((rows, SLOT_PAD, width), lambda i: (0, i, 0)),
        ],
        out_specs=pl.BlockSpec((SLOT_PAD, degrees, width), lambda i: (i, 0, 0)),
        compiler_params=pltpu.CompilerParams(vmem_limit_bytes=40 * 2**20),
        cost_estimate=pl.CostEstimate(
            flops=2 * rows * padded * width * degrees * 8,
            bytes_accessed=4 * slot_count * degrees * width + 4 * rows * padded * width,
            transcendentals=0,
        ),
    )(first_degree, slots, weights, coefs)


def split_two(values):
    top = lax.reduce_precision(values, 8, 7)
    return [top.astype(jnp.bfloat16), (values - top).astype(jnp.bfloat16)]


def pick_points(arrays, index):
    length = arrays[0].shape[0]
    tiles = -(-length // 128)
    matrix = jnp.stack(arrays).reshape(len(arrays), tiles, 128)
    chosen = (jnp.arange(tiles, dtype=jnp.int32)[:, None] == index[None, :] // 128).astype(jnp.bfloat16)
    spread = jnp.einsum("kta,tx->kax", matrix, chosen, preferred_element_type=jnp.float32)
    lane = jnp.arange(128, dtype=jnp.int32)[:, None] == index[None, :] % 128
    return jnp.where(lane[None], spread, 0.0).sum(axis=1)


def shifted(array, axis, count, step):
    pairs = [(i, i + step) for i in range(count) if 0 <= i + step < count]
    return lax.ppermute(array, axis, pairs)


def advance_coupled_model(
    bordered_array,
    meridian_exchange_factor,
    zonal_exchange_factor,
    depthwise_exchange_factor,
    boundary_warming_term,
):
    centre = bordered_array[:, 1:-1]
    meridional = meridian_exchange_factor[1:] * (
        bordered_array[:, 2:] - centre
    ) - meridian_exchange_factor[:-1] * (centre - bordered_array[:, :-2])
    east_flux = zonal_exchange_factor * (jnp.roll(centre, -1, axis=2) - centre)
    zonal_div = east_flux - jnp.roll(east_flux, 1, axis=2)
    vertical_flux = depthwise_exchange_factor * (centre[1:] - centre[:-1])
    zero_layer = jnp.zeros_like(vertical_flux[:1])
    vertical = jnp.concatenate([vertical_flux, zero_layer], 0) - jnp.concatenate(
        [zero_layer, vertical_flux], 0
    )
    forced = jnp.concatenate([boundary_warming_term[None], jnp.zeros_like(centre[1:])], 0)
    return centre + meridional + zonal_div + vertical + forced


def body(
    physical_state,
    parallel_lengths,
    zonal_mode_assignment,
    weighted_associated_polynomials,
    marine_tracer_state,
    lateral_diffusivity,
    depthwise_diffusivity,
    water_indicator,
    overlying_parallel,
    underlying_marine_parallel,
):
    lat_count = lax.axis_size("lat")
    groups = lax.axis_size("sec") * lax.axis_size("col")
    devices = groups * lat_count
    grid_width = physical_state.shape[2]
    strata = physical_state.shape[1] // 4
    slot_count, wave_count, row_count = weighted_associated_polynomials.shape
    block_degrees = wave_count // groups
    padded = -(-slot_count // SLOT_PAD) * SLOT_PAD
    linear_index = (
        lax.axis_index("sec") * lat_count + lax.axis_index("lat")
    ) * lax.axis_size("col") + lax.axis_index("col")
    group_index = lax.axis_index("sec") * lax.axis_size("col") + lax.axis_index("col")
    points = parallel_lengths[0]

    rows = marine_tracer_state.shape[1]
    span = marine_tracer_state.shape[2]
    layers = marine_tracer_state.shape[0]
    sea = water_indicator.astype(jnp.float32)
    relative = (overlying_parallel - linear_index).astype(jnp.float32)
    payload = jnp.concatenate(
        [
            marine_tracer_state,
            lateral_diffusivity[None],
            depthwise_diffusivity[None],
            sea[None],
            jnp.broadcast_to(relative[:, None], (rows, span))[None],
        ],
        axis=0,
    )
    before = shifted(payload, LINE, devices, 1)
    after = shifted(payload, LINE, devices, -1)

    send = weighted_associated_polynomials.reshape(slot_count, groups, block_degrees, row_count)
    send = jnp.transpose(send, (1, 3, 0, 2))
    send = jnp.pad(send, ((0, 0), (0, 0), (0, padded - slot_count), (0, 128 - block_degrees)))
    weights = lax.all_to_all(send, GROUP, split_axis=0, concat_axis=0, tiled=True)
    weights = weights.reshape(groups * row_count, padded, 128)

    slots = zonal_mode_assignment.reshape(lat_count, slot_count)
    slots = jnp.pad(slots, ((0, 0), (0, padded - slot_count)), constant_values=wave_count)
    outgoing = fourier_slots(
        physical_state[0], parallel_lengths, (slots.reshape(-1, 1), wave_count)
    )
    outgoing = outgoing.reshape(lat_count, padded, outgoing.shape[1])
    incoming = lax.all_to_all(outgoing, "lat", split_axis=0, concat_axis=0, tiled=True)
    coefs = lax.all_gather(incoming, GROUP, axis=0, tiled=True)

    surface = jnp.concatenate([before[0], marine_tracer_state[0], after[0]], axis=0)
    under = underlying_marine_parallel[0] - (linear_index - 1) * rows
    skin = jnp.where(jnp.arange(3 * rows)[:, None] == under, surface, 0.0).sum(axis=0)
    ocean_points = jnp.arange(span, dtype=jnp.int32)
    column = ocean_points * points // span
    sea_column = jnp.minimum(column * span // points, span - 1)
    skin_hi, skin_lo = split_two(skin)
    mapped = pick_points([skin_hi, skin_lo], sea_column)
    bottom = strata - 1
    zonal_wind = physical_state[0, bottom].astype(jnp.float32)
    meridional_wind = physical_state[0, strata + bottom].astype(jnp.float32)
    speed = thermal_transfer_factor * jnp.sqrt(
        zonal_wind * zonal_wind + meridional_wind * meridional_wind + 1.0
    )
    speed_hi, speed_lo = split_two(speed)
    picked = pick_points([speed_hi, speed_lo, physical_state[0, 2 * strata + bottom]], column)
    flux = (picked[0] + picked[1]) * (mapped[0] + mapped[1] - picked[2])
    flux_near = {
        step: shifted(flux, LINE, devices, -step) if step else flux for step in (-2, -1, 0, 1, 2)
    }

    whole = jnp.concatenate([before, payload, after], axis=1)
    thermal = whole[:layers]
    kappa, depth, sea, relative = (whole[layers + k] for k in range(4))
    owner = jnp.arange(3 * rows, dtype=jnp.int32)[:, None] // rows - 1
    target = relative + owner.astype(jnp.float32)
    forcing = jnp.zeros_like(sea)
    for step, row in flux_near.items():
        forcing = jnp.where(target == step, row[None], forcing)
    source = force_coef * sea * forcing
    depthwise = depth * sea
    faces = 0.5 * (kappa[:-1] + kappa[1:]) * sea[:-1] * sea[1:]
    east = 0.5 * (kappa + jnp.roll(kappa, -1, axis=1)) * sea * jnp.roll(sea, -1, axis=1)
    total = 3 * rows
    for iteration in range(OSTEPS):
        a, b = iteration + 1, total - iteration - 1
        thermal = advance_coupled_model(
            thermal, faces[a - 1 : b], east[a:b], depthwise[a:b], source[a:b]
        )

    own_waves = lax.dynamic_slice_in_dim(
        slots.reshape(-1), lax.axis_index("lat") * padded, padded
    )
    first_degree = jnp.reshape(group_index * block_degrees, (1,)).astype(jnp.int32)
    harmonic = legendre(weights, coefs, own_waves, first_degree, slot_count, block_degrees)
    return (jnp.transpose(harmonic, (1, 0, 2)), thermal)


def solution(mesh):
    return jax.shard_map(
        body,
        mesh=mesh,
        in_specs=(
            P(LINE, None, None),
            P(LINE),
            P(),
            P("lat", None, GROUP),
            P(None, LINE, None),
            P(LINE, None),
            P(LINE, None),
            P(LINE, None),
            P(LINE),
            P(LINE),
        ),
        out_specs=(P(GROUP, "lat", None), P(None, LINE, None)),
        check_vma=False,
    )
```

time: 743 us -> 110 us (0.15); the launches traced: 728 us -> 110 us
  waiting for transfers between devices: 303 us -> 12.2 us
  other arithmetic: 200 us -> 15.4 us
  local copies, waits for them, and re-layouts: 135 us -> 16.7 us
  matrix products: 29.1 us -> 2.74 us
  Pallas kernels: 0 us -> 18.5 us
  blocking collectives: 14.1 us -> 0 us
    reduce_scatter x1 -> x0, waiting for transfers between devices: 296 us -> none  [body(): lax.psum_scatter(jnp.einsum('snq,qsv->nsv', weighted_associated_polynomia...]
    another operation x2 -> x0, other arithmetic: 177 us -> none
    transpose x1 -> x0, local copies, waits for them, and re-layouts: 69.5 us -> none  [body(): jnp.einsum('snq,qsv->nsv', weighted_associated_polynomials, incoming, pre...]
    gather x5 -> x0, local copies, waits for them, and re-layouts: 54.9 us -> none  [the longest x1 28.8 us: body(): jnp.take_along_axis(skin_warmth_parallels, sea_column_index, axis=1)]
    dot_general x2, matrix products: 29.1 us -> 2.74 us  [pick_points(): jnp.einsum('kta,tx->kax', matrix, chosen, preferred_element_type=jnp.floa...]
    pallas_call x0 -> x2, Pallas kernels: none -> 18.5 us  [the longest x1 9.59 us: legendre(): pl.pallas_call(legendre_kernel, grid=(padded // SLOT_PAD,), out_shape=jax...]
    ppermute x12 -> x6, starting transfers between devices: 30.6 us -> 15.6 us  [shifted(): return lax.ppermute(array, axis, pairs)]
    all_to_all x1 -> x0, blocking collectives: 14.1 us -> none  [body(): lax.all_to_all(outgoing, 'lat', split_axis=1, concat_axis=0, tiled=True)]
  transfers between devices with their start and end apart: 13 -> 9, of which waited for: 5 -> 1; matrix products, arithmetic and copies ran while one was open for 9% -> 26% of each run, Pallas kernels for 0% -> 8%
where the time goes in v1:
time: 110 us
  starting transfers between devices  27.9 us (25%)
  Pallas kernels  18.5 us (17%)
  local copies, waits for them, and re-layouts  16.7 us (15%)
  between operations  16 us (15%)
  other arithmetic  15.4 us (14%)
  waiting for transfers between devices  12.2 us (11%)
  matrix products  2.74 us (2%)
    ppermute x6, starting transfers between devices, shifted(): return lax.ppermute(array, axis, pairs)  15.6 us
    all_gather x1, waiting for transfers between devices, body(): coefs = lax.all_gather(incoming, GROUP, axis=0, tiled=True)  11.5 us
    pallas_call x1, Pallas kernels, legendre(): pl.pallas_call(legendre_kernel, grid=(padded // SLOT_PAD,), out_shape=jax...  9.59 us
    pallas_call x1, Pallas kernels, fourier_slots(): pl.pallas_call(fourier_kernel, out_shape=jax.ShapeDtypeStruct((slots[0].s...  8.94 us
    unnamed x19, local copies, waits for them, and re-layouts  8.61 us
    all_to_all x1, starting transfers between devices, body(): lax.all_to_all(send, GROUP, split_axis=0, concat_axis=0, tiled=True)  6.89 us
    all_to_all x1, starting transfers between devices, body(): lax.all_to_all(outgoing, 'lat', split_axis=0, concat_axis=0, tiled=True)  5.44 us
    add x4, other arithmetic, advance_coupled_model(): return centre + meridional + zonal_div + vertical + forced  4.07 us
  transfers between devices with their start and end apart: 9, of which 1 were waited for; matrix products, arithmetic and copies ran while one was open for 26% of the time, Pallas kernels for 8%

profile of v1, /device:TPU:0, one launch (start us, length us, event | category | flops | bytes accessed | tf_op | source)
XLA Modules:
  0.0 109.5 jit_solution(15399081002419826208)
XLA Ops:
  7.2 1.1 %constant_dynamic-update-slice_fusion = f32[12,4,4096]{2,1,0:T(4,128)S(1)} fusion(f32[8,4,4096]{2,1,0:T(4,128)} %param.14), kind=kLoop, calls=%fused_computation.159 | loop fusion | bytes 1048576
  11.7 1.3 %collective-permute-start.1 = (f32[12,4,4096]{2,1,0:T(4,128)S(1)}, f32[12,4,4096]{2,1,0:T(4,128)}, u32[]{:S(2)}, u32[]{:S(2)}) collective-permute-start(f32[12,4,4096]{2,1,0:T(4,128)S(1)} %broadcast_dynamic-update-slice_fusion), channel_id=1, source_target_pairs={{1,0},{2,1},{3,2},{4,3},{5,4},{6,5},{7,6},{8,7},{9,8},{10,9},{11,1... | collective-permute-start | bytes 2359304 | tf_op jit(solution)/shard_map/ppermute | solution.py:166
  13.0 3.9 %collective-permute-start = (f32[12,4,4096]{2,1,0:T(4,128)S(1)}, f32[12,4,4096]{2,1,0:T(4,128)}, u32[]{:S(2)}, u32[]{:S(2)}) collective-permute-start(f32[12,4,4096]{2,1,0:T(4,128)S(1)} %broadcast_dynamic-update-slice_fusion), channel_id=1, source_target_pairs={{0,1},{1,2},{2,3},{3,4},{4,5},{5,6},{6,7},{7,8},{8,9},{9,10},{10,1... | collective-permute-start | bytes 2359304 | tf_op jit(solution)/shard_map/ppermute | solution.py:166
  19.6 8.9 %shard_map.113 = bf16[896,128]{1,0:T(8,128)(2,1)} custom-call(s32[1]{0:T(128)} %copy.24.points_ref, f32[2,60,640]{2,1,0:T(8,128)S(1)} %maximum_multiply_fusion.table_ref, s32[896,1]{1,0:T(8,128)S(1)} %reshape.484.slots_ref, bf16[64,5120]{1,0:T(8,128)(2,1)S(1)} %bitcast.90), custom_call_target="tpu_custom_call" | custom-call | flops 838860800 | bytes 4194304 | tf_op jit(solution)/shard_map/pallas_call | solution.py:88
  28.6 5.4 %all-to-all-start.1 = ((bf16[4,224,128]{2,1,0:T(8,128)(2,1)}), bf16[4,224,128]{2,1,0:T(8,128)(2,1)S(1)}, u32[]{:S(2)}, u32[]{:S(2)}) async-start(bf16[4,224,128]{2,1,0:T(8,128)(2,1)} %bitcast.6), calls=%async_computation.1 | async-start | bytes 458752 | tf_op jit(solution)/shard_map/all_to_all | solution.py:247
  36.0 1.1 iota_compare_fusion
  37.7 1.1 iota_compare_fusion.1
  38.7 2.3 %copy.16 = bf16[214,640,4]{0,1,2:T(8,128)(2,1)} copy(bf16[214,640,4]{1,2,0:T(4,128)(2,1)S(1)} %copy-done.2) | data formatting | bytes 2191360 | tf_op args[3]
  41.0 1.9 %copy.19 = bf16[8,4,214,80]{3,2,1,0:T(8,128)(2,1)S(1)} copy(bf16[8,4,214,80]{2,3,0,1:T(8,128)(2,1)} %bitcast.95) | data formatting | bytes 2191360
  43.1 1.6 %pad.21.clone = bf16[8,4,224,128]{3,2,1,0:T(8,128)(2,1)} pad(bf16[8,4,214,80]{3,2,1,0:T(8,128)(2,1)S(1)} %copy.19, bf16[]{:T(256)} %constant.117.clone.1), padding=0_0x0_0x0_10x0_48 | pad | bytes 2930690 | tf_op jit(solution)/shard_map/jit(_pad)/pad | solution.py:237
  44.8 1.8 %select_reduce_fusion = f32[3,4096]{1,0:T(4,128)} fusion(pred[128,4096]{1,0:T(8,128)(4,1)S(1)} %copy-done.5, s32[4096]{0:T(1024)S(1)} %copy-done.6, bf16[1,40,128]{2,1,0:T(8,128)(2,1)S(1)} %bitcast.103, bf16[1,40,128]{2,1,0:T(8,128)(2,1)S(1)} %get-tuple-element.16, bf16[1,40,128]{2,1,0:T(8,128)(2,1)S(1)} %get-tuple-element.15), kind=kOutput, calls=%fused_computation | convolution fusion | flops 129157120 | bytes 620544 | tf_op jit(solution)/shard_map/kta,tx->kax/dot_general | solution.py:159
  46.6 6.9 %all-to-all-start = ((bf16[8,4,224,128]{3,2,1,0:T(8,128)(2,1)}), bf16[8,4,224,128]{3,2,1,0:T(8,128)(2,1)S(1)}, u32[]{:S(2)}, u32[]{:S(2)}) async-start(bf16[8,4,224,128]{3,2,1,0:T(8,128)(2,1)} %pad.21.clone), calls=%async_computation | async-start | bytes 3670016 | tf_op jit(solution)/shard_map/all_to_all | solution.py:238
  57.0 1.0 fusion.62
  58.0 1.3 %collective-permute-start.2 = (f32[4096]{0:T(1024)S(1)}, f32[4096]{0:T(1024)S(1)}, u32[]{:S(2)}, u32[]{:S(2)}) collective-permute-start(f32[4096]{0:T(1024)S(1)} %bitcast.98), channel_id=1, source_target_pairs={{2,0},{3,1},{4,2},{5,3},{6,4},{7,5},{8,6},{9,7},{10,8},{11,9},{12,... | collective-permute-start | bytes 49160 | tf_op jit(solution)/shard_map/ppermute | solution.py:166
  59.3 1.3 %collective-permute-start.3 = (f32[4096]{0:T(1024)S(1)}, f32[4096]{0:T(1024)S(1)}, u32[]{:S(2)}, u32[]{:S(2)}) collective-permute-start(f32[4096]{0:T(1024)S(1)} %bitcast.99), channel_id=1, source_target_pairs={{1,0},{2,1},{3,2},{4,3},{5,4},{6,5},{7,6},{8,7},{9,8},{10,9},{11,1... | collective-permute-start | bytes 49160 | tf_op jit(solution)/shard_map/ppermute | solution.py:166
  60.6 3.0 %collective-permute-start.4 = (f32[4096]{0:T(1024)S(1)}, f32[4096]{0:T(1024)S(1)}, u32[]{:S(2)}, u32[]{:S(2)}) collective-permute-start(f32[4096]{0:T(1024)S(1)} %bitcast.100), channel_id=1, source_target_pairs={{0,1},{1,2},{2,3},{3,4},{4,5},{5,6},{6,7},{7,8},{8,9},{9,10},{10,1... | collective-permute-start | bytes 49160 | tf_op jit(solution)/shard_map/ppermute | solution.py:166
  63.7 4.7 %collective-permute-start.5 = (f32[4096]{0:T(1024)S(1)}, f32[4096]{0:T(1024)S(1)}, u32[]{:S(2)}, u32[]{:S(2)}) collective-permute-start(f32[4096]{0:T(1024)S(1)} %bitcast.101), channel_id=1, source_target_pairs={{0,2},{1,3},{2,4},{3,5},{4,6},{5,7},{6,8},{7,9},{8,10},{9,11},{10,... | collective-permute-start | bytes 49160 | tf_op jit(solution)/shard_map/ppermute | solution.py:166
  68.4 1.9 %pad_maximum_fusion = f32[12,12,4096]{2,1,0:T(8,128)S(1)} fusion(f32[12,4,4096]{2,1,0:T(4,128)} %collective-permute-done.1, f32[12,4,4096]{2,1,0:T(4,128)S(1)} %broadcast_dynamic-update-slice_fusion, f32[12,4,4096]{2,1,0:T(4,128)} %collective-permute-done), kind=kLoop, calls=%fused_computation.2 | loop fusion | flops 1179648 | bytes 4718592 | tf_op jit(solution)/shard_map/concatenate | solution.py:271
  72.1 1.1 %fusion.2 = f32[8,10,4096]{2,1,0:T(8,128)S(1)} fusion(f32[12,4,4096]{2,1,0:T(4,128)} %collective-permute-done.1, f32[12,4,4096]{2,1,0:T(4,128)S(1)} %broadcast_dynamic-update-slice_fusion, f32[12,4,4096]{2,1,0:T(4,128)} %collective-permute-done, f32[8,10,4095]{2,1,0:T(8,128)S(1)} %slice.419, f32[12,12,4096]{2,1,0:T(8,128)S(1)} %pad_maximum_fusion, ...), kind=kLoop, calls=%fused_computation.6 | loop fusion | flops 1638400 | bytes 6454976 | tf_op jit(solution)/shard_map/mul | solution.py:180
  73.4 1.5 %fusion.8 = f32[8,10,4096]{2,1,0:T(8,128)S(1)} fusion(f32[12,12,4096]{2,1,0:T(8,128)S(1)} %pad_maximum_fusion, f32[8,10,4096]{2,1,0:T(8,128)S(1)} %fusion.2, f32[8,10,4095]{2,1,0:T(8,128)S(1)} %bitcast.91, f32[8,10,1]{2,1,0:T(8,128)S(1)} %slice.420, f32[1,10,4096]{2,1,0:T(8,128)S(1)} %slice_bitcast_fusion, f32[7,10,4096]{2,1,0:T(8,128)S(1)} %fusion.10, ...), kind=kLoop, calls=%fused_computation.14 | loop fusion | flops 3932160 | bytes 9502720 | tf_op jit(solution)/shard_map/add | solution.py:188
  78.7 1.4 %fusion.37 = f32[8,4,4096]{2,1,0:T(4,128)} fusion(f32[8,6,4096]{2,1,0:T(8,128)S(1)} %fusion.17, f32[8,4,4096]{2,1,0:T(4,128)S(1)} %fusion.39, f32[8,4,4095]{2,1,0:T(4,128)S(1)} %bitcast.96, f32[8,4,1]{2,1,0:T(4,128)S(1)} %slice.471, f32[1,4,4096]{2,1,0:T(4,128)S(1)} %slice_bitcast_fusion.13, f32[7,4,4096]{2,1,0:T(4,128)S(1)} %fusion.42, ...), kind=kLoop, calls=%fused_computation.59 | loop fusion | flops 1572864 | bytes 3801088 | tf_op jit(solution)/shard_map/add | solution.py:188
  80.0 11.5 %all-gather.2.cloned.1.call-done.coef_ref = bf16[32,224,128]{2,1,0:T(8,128)(2,1)} async-done(((bf16[4,224,128]{2,1,0:T(8,128)(2,1)}), bf16[32,224,128]{2,1,0:T(8,128)(2,1)}) %all-gather.2.cloned.1.call-update) | async-done | bytes 1835024 | tf_op jit(solution)/shard_map/all_gather | solution.py:248
  91.6 1.5 %copy-done = bf16[32,224,128]{2,1,0:T(8,128)(2,1)S(1)} copy-done((bf16[32,224,128]{2,1,0:T(8,128)(2,1)S(1)}, bf16[32,224,128]{2,1,0:T(8,128)(2,1)}, u32[]{:S(2)}) %copy-start) | copy-done | bytes 1835032
  93.1 9.6 %shard_map.114 = f32[214,80,128]{2,1,0:T(8,128)} custom-call(s32[1]{0:T(128)} %bitcast.degree_ref, s32[224]{0:T(256)S(1)} %dynamic_slice.3.slots_ref, bf16[32,224,128]{2,1,0:T(8,128)(2,1)S(1)} %bitcast.89, bf16[32,224,128]{2,1,0:T(8,128)(2,1)S(1)} %copy-done), custom_call_target="tpu_custom_call" | custom-call | flops 1174405120 | bytes 12435456 | tf_op jit(solution)/shard_map/pallas_call | solution.py:129
  (96 shorter events, 16.2 us)
Async XLA Ops:
  7.2 12.5 %copy-start.1 = (bf16[1,64,5120]{2,1,0:T(8,128)(2,1)S(1)}, bf16[1,64,5120]{2,1,0:T(8,128)(2,1)}, u32[]{:S(2)}) copy-start(bf16[1,64,5120]{2,1,0:T(8,128)(2,1)} %param.10) | copy-start | bytes 1966084
  11.7 42.6 %collective-permute-start.1 = (f32[12,4,4096]{2,1,0:T(4,128)S(1)}, f32[12,4,4096]{2,1,0:T(4,128)}, u32[]{:S(2)}, u32[]{:S(2)}) collective-permute-start(f32[12,4,4096]{2,1,0:T(4,128)S(1)} %broadcast_dynamic-update-slice_fusion), channel_id=1, source_target_pairs={{1,0},{2,1},{3,2},{4,3},{5,4},{6,5},{7,6},{8,7},{9,8},{10,9},{11,1... | collective-permute-start | bytes 2359304 | tf_op jit(solution)/shard_map/ppermute | solution.py:166
  13.0 42.2 %collective-permute-start = (f32[12,4,4096]{2,1,0:T(4,128)S(1)}, f32[12,4,4096]{2,1,0:T(4,128)}, u32[]{:S(2)}, u32[]{:S(2)}) collective-permute-start(f32[12,4,4096]{2,1,0:T(4,128)S(1)} %broadcast_dynamic-update-slice_fusion), channel_id=1, source_target_pairs={{0,1},{1,2},{2,3},{3,4},{4,5},{5,6},{6,7},{7,8},{8,9},{9,10},{10,1... | collective-permute-start | bytes 2359304 | tf_op jit(solution)/shard_map/ppermute | solution.py:166
  19.6 19.1 %copy-start.2 = (bf16[214,640,4]{1,2,0:T(4,128)(2,1)S(1)}, bf16[214,640,4]{1,2,0:T(4,128)(2,1)}, u32[]{:S(2)}) copy-start(bf16[214,640,4]{1,2,0:T(4,128)(2,1)} %param.13) | copy-start | bytes 3287044
  28.6 18.1 %all-to-all-start.1 = ((bf16[4,224,128]{2,1,0:T(8,128)(2,1)}), bf16[4,224,128]{2,1,0:T(8,128)(2,1)S(1)}, u32[]{:S(2)}, u32[]{:S(2)}) async-start(bf16[4,224,128]{2,1,0:T(8,128)(2,1)} %bitcast.6), calls=%async_computation.1 | async-start | bytes 458752 | tf_op jit(solution)/shard_map/all_to_all | solution.py:247
  43.1 1.7 %copy-start.5 = (pred[128,4096]{1,0:T(8,128)(4,1)S(1)}, pred[128,4096]{1,0:T(8,128)(4,1)}, u32[]{:S(2)}) copy-start(pred[128,4096]{1,0:T(8,128)(4,1)} %iota_compare_fusion.1) | copy-start | bytes 1572868
  43.1 1.7 %copy-start.6 = (s32[4096]{0:T(1024)S(1)}, s32[4096]{0:T(1024)}, u32[]{:S(2)}) copy-start(s32[4096]{0:T(1024)} %get-tuple-element.23) | copy-start | bytes 49156
  46.6 6.9 %copy-start.3 = (bf16[4,224,128]{2,1,0:T(8,128)(2,1)}, bf16[4,224,128]{2,1,0:T(8,128)(2,1)S(1)}, u32[]{:S(2)}) copy-start(bf16[4,224,128]{2,1,0:T(8,128)(2,1)S(1)} %all-to-all-done.1) | copy-start | bytes 688132
  46.6 9.5 %copy-start.4 = (pred[128,4096]{1,0:T(8,128)(4,1)S(1)}, pred[128,4096]{1,0:T(8,128)(4,1)}, u32[]{:S(2)}) copy-start(pred[128,4096]{1,0:T(8,128)(4,1)} %iota_compare_fusion) | copy-start | bytes 1572868
  46.6 33.4 %all-to-all-start = ((bf16[8,4,224,128]{3,2,1,0:T(8,128)(2,1)}), bf16[8,4,224,128]{3,2,1,0:T(8,128)(2,1)S(1)}, u32[]{:S(2)}, u32[]{:S(2)}) async-start(bf16[8,4,224,128]{3,2,1,0:T(8,128)(2,1)} %pad.21.clone), calls=%async_computation | async-start | bytes 3670016 | tf_op jit(solution)/shard_map/all_to_all | solution.py:238
  53.5 38.0 %all-gather.2.cloned.1.call-start = ((), (), s32[]{:S(2)}) async-start(), calls=%async_computation.2 | async-start | bytes 2064384 | tf_op jit(solution)/shard_map/all_gather | solution.py:248
  58.0 13.5 %collective-permute-start.2 = (f32[4096]{0:T(1024)S(1)}, f32[4096]{0:T(1024)S(1)}, u32[]{:S(2)}, u32[]{:S(2)}) collective-permute-start(f32[4096]{0:T(1024)S(1)} %bitcast.98), channel_id=1, source_target_pairs={{2,0},{3,1},{4,2},{5,3},{6,4},{7,5},{8,6},{9,7},{10,8},{11,9},{12,... | collective-permute-start | bytes 49160 | tf_op jit(solution)/shard_map/ppermute | solution.py:166
  59.3 12.2 %collective-permute-start.3 = (f32[4096]{0:T(1024)S(1)}, f32[4096]{0:T(1024)S(1)}, u32[]{:S(2)}, u32[]{:S(2)}) collective-permute-start(f32[4096]{0:T(1024)S(1)} %bitcast.99), channel_id=1, source_target_pairs={{1,0},{2,1},{3,2},{4,3},{5,4},{6,5},{7,6},{8,7},{9,8},{10,9},{11,1... | collective-permute-start | bytes 49160 | tf_op jit(solution)/shard_map/ppermute | solution.py:166
  60.6 10.9 %collective-permute-start.4 = (f32[4096]{0:T(1024)S(1)}, f32[4096]{0:T(1024)S(1)}, u32[]{:S(2)}, u32[]{:S(2)}) collective-permute-start(f32[4096]{0:T(1024)S(1)} %bitcast.100), channel_id=1, source_target_pairs={{0,1},{1,2},{2,3},{3,4},{4,5},{5,6},{6,7},{7,8},{8,9},{9,10},{10,1... | collective-permute-start | bytes 49160 | tf_op jit(solution)/shard_map/ppermute | solution.py:166
  63.7 7.9 %collective-permute-start.5 = (f32[4096]{0:T(1024)S(1)}, f32[4096]{0:T(1024)S(1)}, u32[]{:S(2)}, u32[]{:S(2)}) collective-permute-start(f32[4096]{0:T(1024)S(1)} %bitcast.101), channel_id=1, source_target_pairs={{0,2},{1,3},{2,4},{3,5},{4,6},{5,7},{6,8},{7,9},{8,10},{9,11},{10,... | collective-permute-start | bytes 49160 | tf_op jit(solution)/shard_map/ppermute | solution.py:166
  91.6 1.5 %copy-start = (bf16[32,224,128]{2,1,0:T(8,128)(2,1)S(1)}, bf16[32,224,128]{2,1,0:T(8,128)(2,1)}, u32[]{:S(2)}) copy-start(bf16[32,224,128]{2,1,0:T(8,128)(2,1)} %all-gather.2.cloned.1.call-done.coef_ref) | copy-start | bytes 5505028
Sparse Core Ops, SparseCore 0:
  56.3 35.2 all-gather.1

commit v2 on v1

--- a/solution.py
+++ b/solution.py
@@ -33,7 +33,117 @@
     return jnp.stack([jnp.cos(angle), -jnp.sin(angle)]) * scale[None, :, None]
 
 
-def fourier_kernel(points_ref, table_ref, slots_ref, x_ref, out_ref, base_ref, acc_ref):
+MESH = pl.DeviceIdType.MESH
+
+
+def place_of(index, lat_count, col_count):
+    return {
+        "sec": index // (lat_count * col_count),
+        "lat": index // col_count % lat_count,
+        "col": index % col_count,
+    }
+
+
+def exchange_kernel(
+    sizes,
+    points_ref,
+    table_ref,
+    slots_ref,
+    x_ref,
+    weight_ref,
+    *refs,
+):
+    sec_count, lat_count, col_count = sizes
+    halo = refs[:5]
+    coef_out, weight_out = refs[5:7]
+    before, after = refs[7:12], refs[12:17]
+    (base_ref, acc_ref, mine_ref, local_sem, weight_send, weight_recv, halo_send, halo_recv,
+     lat_send, lat_recv, group_send, group_recv) = refs[17:]
+    groups = sec_count * col_count
+    devices = groups * lat_count
+    sec, lat, col = (lax.axis_index(name) for name in LINE)
+    group = sec * col_count + col
+    line = (sec * lat_count + lat) * col_count + col
+    following = place_of((line + 1) % devices, lat_count, col_count)
+    previous = place_of((line + devices - 1) % devices, lat_count, col_count)
+
+    def group_place(step):
+        other = (group + step) % groups
+        return other, {"sec": other // col_count, "lat": lat, "col": other % col_count}
+
+    def lat_place(step):
+        other = (lat + step) % lat_count
+        return other, {"sec": sec, "lat": other, "col": col}
+
+    barrier = pltpu.get_barrier_semaphore()
+    for place in (following, previous):
+        pl.semaphore_signal(barrier, inc=1, device_id=place, device_id_type=MESH)
+
+    @pl.loop(1, groups)
+    def _(step):
+        pl.semaphore_signal(barrier, inc=1, device_id=group_place(step)[1], device_id_type=MESH)
+
+    @pl.loop(1, lat_count)
+    def _(step):
+        pl.semaphore_signal(barrier, inc=1, device_id=lat_place(step)[1], device_id_type=MESH)
+
+    pl.semaphore_wait(barrier, groups + lat_count)
+
+    def weight_copy(step):
+        other, place = group_place(step)
+        return pltpu.make_async_remote_copy(
+            src_ref=weight_ref.at[other],
+            dst_ref=weight_out.at[group],
+            send_sem=weight_send.at[step],
+            recv_sem=weight_recv.at[step],
+            device_id=place,
+            device_id_type=MESH,
+        )
+
+    def halo_copies():
+        return [
+            pltpu.make_async_remote_copy(
+                src_ref=halo[k],
+                dst_ref=target[k],
+                send_sem=halo_send.at[side, k],
+                recv_sem=halo_recv.at[side, k],
+                device_id=place,
+                device_id_type=MESH,
+            )
+            for k in range(5)
+            for side, (target, place) in enumerate(((before, following), (after, previous)))
+        ]
+
+    def lat_copy(step):
+        other, place = lat_place(step)
+        return pltpu.make_async_remote_copy(
+            src_ref=mine_ref.at[other],
+            dst_ref=coef_out.at[group, lat],
+            send_sem=lat_send.at[step],
+            recv_sem=lat_recv.at[step],
+            device_id=place,
+            device_id_type=MESH,
+        )
+
+    def group_copy(step):
+        return pltpu.make_async_remote_copy(
+            src_ref=coef_out.at[group],
+            dst_ref=coef_out.at[group],
+            send_sem=group_send.at[step],
+            recv_sem=group_recv.at[step],
+            device_id=group_place(step)[1],
+            device_id_type=MESH,
+        )
+
+    for copy in halo_copies():
+        copy.start()
+    own_weights = pltpu.make_async_copy(weight_ref.at[group], weight_out.at[group], local_sem.at[0])
+    own_weights.start()
+
+    @pl.loop(1, groups)
+    def _(step):
+        weight_copy(step).start()
+
     points = points_ref[0]
     waves = table_ref.shape[2]
     fields = x_ref.shape[0]
@@ -68,42 +178,93 @@
 
     wave = lax.broadcasted_iota(jnp.int32, acc_ref.shape, 1)
     coefs = jnp.where(wave < points // 2, acc_ref[...], 0.0).astype(jnp.bfloat16)
-    rows = 112 if slots_ref.shape[0] % 112 == 0 else slots_ref.shape[0] // 8
-
-    @pl.loop(0, slots_ref.shape[0] // rows)
-    def _(b):
-        start = pl.multiple_of(b * rows, 16)
-        held = slots_ref[pl.ds(start, rows)]
-        pick = held == lax.broadcasted_iota(jnp.int32, (rows, waves), 1)
+    padded = mine_ref.shape[1]
+
+    def fill(other):
+        held = slots_ref[pl.ds(pl.multiple_of(other * padded, 16), padded)]
+        pick = held == lax.broadcasted_iota(jnp.int32, (padded, waves), 1)
         pick = jnp.where(pick, 1.0, 0.0).astype(jnp.bfloat16)
-        out_ref[pl.ds(start, rows)] = lax.dot_general(
+        mine_ref[other] = lax.dot_general(
             pick, coefs, (((1,), (1,)), ((), ())), preferred_element_type=jnp.float32
         ).astype(jnp.bfloat16)
 
-
-def fourier_slots(state, points, slots):
+    @pl.loop(1, lat_count)
+    def _(step):
+        fill((lat + step) % lat_count)
+        lat_copy(step).start()
+
+    fill(lat)
+    own_coefs = pltpu.make_async_copy(mine_ref.at[lat], coef_out.at[group, lat], local_sem.at[1])
+    own_coefs.start()
+    own_coefs.wait()
+
+    @pl.loop(1, lat_count)
+    def _(step):
+        lat_copy(step).wait_recv()
+
+    @pl.loop(1, groups)
+    def _(step):
+        group_copy(step).start()
+
+    for copy in halo_copies():
+        copy.wait()
+    own_weights.wait()
+
+    @pl.loop(1, groups)
+    def _(step):
+        weight_copy(step).wait()
+
+    @pl.loop(1, lat_count)
+    def _(step):
+        lat_copy(step).wait_send()
+
+    @pl.loop(1, groups)
+    def _(step):
+        group_copy(step).wait()
+
+
+def exchange(sizes, points, table, slots, state, weights, halo):
     fields, width = state.shape
-    waves = slots[1]
-    table = angle_tables(points[0], waves, width)
-    return pl.pallas_call(
-        fourier_kernel,
-        out_shape=jax.ShapeDtypeStruct((slots[0].shape[0], 2 * fields), jnp.bfloat16),
-        in_specs=[
-            pl.BlockSpec(memory_space=pltpu.SMEM),
-            pl.BlockSpec(memory_space=pltpu.VMEM),
-            pl.BlockSpec(memory_space=pltpu.VMEM),
-            pl.BlockSpec(memory_space=pltpu.VMEM),
-        ],
-        out_specs=pl.BlockSpec(memory_space=pltpu.VMEM),
+    waves = table.shape[2]
+    sec_count, lat_count, col_count = sizes
+    groups = sec_count * col_count
+    padded = weights.shape[2]
+    anywhere = pl.BlockSpec(memory_space=pl.ANY)
+    inside = pl.BlockSpec(memory_space=pltpu.VMEM)
+    halo_shapes = [jax.ShapeDtypeStruct(part.shape, part.dtype) for part in halo]
+    out = pl.pallas_call(
+        functools.partial(exchange_kernel, sizes),
+        out_shape=[
+            jax.ShapeDtypeStruct((groups, lat_count, padded, 2 * fields), jnp.bfloat16),
+            jax.ShapeDtypeStruct(weights.shape, jnp.bfloat16),
+        ]
+        + halo_shapes
+        + halo_shapes,
+        in_specs=[pl.BlockSpec(memory_space=pltpu.SMEM), inside, inside, inside, anywhere]
+        + [anywhere] * 5,
+        out_specs=[anywhere] * 12,
         scratch_shapes=[
             pltpu.VMEM((2, CHUNK, waves), jnp.float32),
             pltpu.VMEM((2 * fields, waves), jnp.float32),
+            pltpu.VMEM((lat_count, padded, 2 * fields), jnp.bfloat16),
+            pltpu.SemaphoreType.DMA((2,)),
+            pltpu.SemaphoreType.DMA((groups,)),
+            pltpu.SemaphoreType.DMA((groups,)),
+            pltpu.SemaphoreType.DMA((2, 5)),
+            pltpu.SemaphoreType.DMA((2, 5)),
+            pltpu.SemaphoreType.DMA((lat_count,)),
+            pltpu.SemaphoreType.DMA((lat_count,)),
+            pltpu.SemaphoreType.DMA((groups,)),
+            pltpu.SemaphoreType.DMA((groups,)),
         ],
-        compiler_params=pltpu.CompilerParams(vmem_limit_bytes=32 * 2**20),
+        compiler_params=pltpu.CompilerParams(
+            vmem_limit_bytes=24 * 2**20, collective_id=0, has_side_effects=True
+        ),
         cost_estimate=pl.CostEstimate(
-            flops=4 * fields * waves * width, bytes_accessed=4 * 2**20, transcendentals=0
+            flops=4 * fields * waves * width, bytes_accessed=8 * 2**20, transcendentals=0
         ),
-    )(points, table, slots[0], state)
+    )(points, table, slots, state, weights, *halo)
+    return out[0], out[1], out[2:7], out[7:12]
 
 
 def legendre_kernel(degree_ref, slots_ref, weight_ref, coef_ref, out_ref):
@@ -116,12 +277,12 @@
         values = values.T[:degrees]
         lane_slot = lax.broadcasted_iota(jnp.int32, (degrees, rows * 8), 1) % 8
         coefs = coef_ref[:, cut, :].astype(jnp.float32).reshape(rows * 8, width).astype(jnp.bfloat16)
-        degree = first + lax.broadcasted_iota(jnp.int32, (degrees, rows * 8), 0)
+        degree = first + lax.broadcasted_iota(jnp.int32, (degrees, width), 0)
         for s in range(8):
             wave = slots_ref[pl.program_id(0) * pair + half * 8 + s]
-            keep = (lane_slot == s) & (degree >= wave)
-            left = jnp.where(keep, values, 0.0).astype(jnp.bfloat16)
-            out_ref[half * 8 + s] = jnp.dot(left, coefs, preferred_element_type=jnp.float32)
+            left = jnp.where(lane_slot == s, values, 0.0).astype(jnp.bfloat16)
+            summed = jnp.dot(left, coefs, preferred_element_type=jnp.float32)
+            out_ref[half * 8 + s] = jnp.where(degree >= wave, summed, 0.0)
 
 
 def legendre(weights, coefs, slots, first_degree, slot_count, degrees):
@@ -217,37 +378,36 @@
     rows = marine_tracer_state.shape[1]
     span = marine_tracer_state.shape[2]
     layers = marine_tracer_state.shape[0]
-    sea = water_indicator.astype(jnp.float32)
-    relative = (overlying_parallel - linear_index).astype(jnp.float32)
-    payload = jnp.concatenate(
-        [
-            marine_tracer_state,
-            lateral_diffusivity[None],
-            depthwise_diffusivity[None],
-            sea[None],
-            jnp.broadcast_to(relative[:, None], (rows, span))[None],
-        ],
-        axis=0,
-    )
-    before = shifted(payload, LINE, devices, 1)
-    after = shifted(payload, LINE, devices, -1)
+    relative = overlying_parallel - linear_index
+    halo = [
+        marine_tracer_state,
+        lateral_diffusivity,
+        depthwise_diffusivity,
+        water_indicator,
+        jnp.broadcast_to(jnp.tile(relative, 2)[:, None], (2 * rows, 128)),
+    ]
 
     send = weighted_associated_polynomials.reshape(slot_count, groups, block_degrees, row_count)
     send = jnp.transpose(send, (1, 3, 0, 2))
     send = jnp.pad(send, ((0, 0), (0, 0), (0, padded - slot_count), (0, 128 - block_degrees)))
-    weights = lax.all_to_all(send, GROUP, split_axis=0, concat_axis=0, tiled=True)
-    weights = weights.reshape(groups * row_count, padded, 128)
-
     slots = zonal_mode_assignment.reshape(lat_count, slot_count)
     slots = jnp.pad(slots, ((0, 0), (0, padded - slot_count)), constant_values=wave_count)
-    outgoing = fourier_slots(
-        physical_state[0], parallel_lengths, (slots.reshape(-1, 1), wave_count)
-    )
-    outgoing = outgoing.reshape(lat_count, padded, outgoing.shape[1])
-    incoming = lax.all_to_all(outgoing, "lat", split_axis=0, concat_axis=0, tiled=True)
-    coefs = lax.all_gather(incoming, GROUP, axis=0, tiled=True)
-
-    surface = jnp.concatenate([before[0], marine_tracer_state[0], after[0]], axis=0)
+    coefs, weights, before, after = exchange(
+        (lax.axis_size("sec"), lat_count, lax.axis_size("col")),
+        parallel_lengths,
+        angle_tables(points, wave_count, grid_width),
+        slots.reshape(-1, 1),
+        physical_state[0],
+        send,
+        halo,
+    )
+    coefs = coefs.reshape(groups * lat_count, padded, coefs.shape[3])
+    weights = weights.reshape(groups * row_count, padded, 128)
+    first, last = linear_index == 0, linear_index == devices - 1
+    before = [jnp.where(first, jnp.zeros_like(part), part) for part in before]
+    after = [jnp.where(last, jnp.zeros_like(part), part) for part in after]
+
+    surface = jnp.concatenate([before[0][0], marine_tracer_state[0], after[0][0]], axis=0)
     under = underlying_marine_parallel[0] - (linear_index - 1) * rows
     skin = jnp.where(jnp.arange(3 * rows)[:, None] == under, surface, 0.0).sum(axis=0)
     ocean_points = jnp.arange(span, dtype=jnp.int32)
@@ -268,11 +428,14 @@
         step: shifted(flux, LINE, devices, -step) if step else flux for step in (-2, -1, 0, 1, 2)
     }
 
-    whole = jnp.concatenate([before, payload, after], axis=1)
-    thermal = whole[:layers]
-    kappa, depth, sea, relative = (whole[layers + k] for k in range(4))
+    thermal = jnp.concatenate([before[0], marine_tracer_state, after[0]], axis=1)
+    kappa, depth, sea = (
+        jnp.concatenate([before[k], halo[k], after[k]], axis=0) for k in (1, 2, 3)
+    )
+    sea = sea.astype(jnp.float32)
+    relative = jnp.concatenate([before[4][:rows, :1], relative[:, None], after[4][:rows, :1]], axis=0)
     owner = jnp.arange(3 * rows, dtype=jnp.int32)[:, None] // rows - 1
-    target = relative + owner.astype(jnp.float32)
+    target = relative + owner
     forcing = jnp.zeros_like(sea)
     for step, row in flux_near.items():
         forcing = jnp.where(target == step, row[None], forcing)

time: 110 us -> 131 us (1.19); the launches traced: 110 us -> 128 us
  Pallas kernels: 18.5 us -> 62.7 us
  starting transfers between devices: 27.9 us -> 11.8 us
  between operations: 16 us -> 2.65 us
  waiting for transfers between devices: 12.2 us -> 0.01 us
  local copies, waits for them, and re-layouts: 16.7 us -> 27.7 us
  other arithmetic: 15.4 us -> 21.5 us
    pallas_call x1, Pallas kernels: 8.94 us -> 53.1 us  [exchange(): pl.pallas_call(functools.partial(exchange_kernel, sizes), out_shape=[jax....]
    all_to_all x2 -> x0, starting transfers between devices: 12.3 us -> none  [the longest x1 6.89 us: body(): lax.all_to_all(send, GROUP, split_axis=0, concat_axis=0, tiled=True)]
    all_gather x1 -> x0, waiting for transfers between devices: 11.5 us -> none  [body(): coefs = lax.all_gather(incoming, GROUP, axis=0, tiled=True)]
    ppermute x6 -> x4, starting transfers between devices: 15.6 us -> 11.8 us  [shifted(): return lax.ppermute(array, axis, pairs)]
    slice x7, local copies, waits for them, and re-layouts: 1.66 us -> 4.56 us  [advance_coupled_model(): east_flux = zonal_exchange_factor * (jnp.roll(centre, -1, axis=2) - centre)]
    mul x4, other arithmetic: 1.75 us -> 4.59 us  [advance_coupled_model(): east_flux = zonal_exchange_factor * (jnp.roll(centre, -1, axis=2) - centre)]
    slice x4, local copies, waits for them, and re-layouts: 0.11 us -> 2.92 us  [advance_coupled_model(): meridian_exchange_factor[1:] * (bordered_array[:, 2:] - centre)]
    reshape x0 -> x1, local copies, waits for them, and re-layouts: none -> 1.99 us  [body(): weighted_associated_polynomials.reshape(slot_count, groups, block_degrees...]
  transfers between devices with their start and end apart: 9 -> 4, of which waited for: 1 -> 0; matrix products, arithmetic and copies ran while one was open for 26% -> 15% of each run, Pallas kernels for 8% -> 7%
where the time goes in v2:
time: 131 us; the launch traced here: 128 us
  Pallas kernels  62.7 us (48%)
  local copies, waits for them, and re-layouts  27.7 us (21%)
  other arithmetic  21.5 us (16%)
  starting transfers between devices  11.8 us (9%)
  between operations  2.65 us (2%)
  matrix products  2.12 us (2%)
    pallas_call x1, Pallas kernels, exchange(): pl.pallas_call(functools.partial(exchange_kernel, sizes), out_shape=[jax....  53.1 us
    ppermute x4, starting transfers between devices, shifted(): return lax.ppermute(array, axis, pairs)  11.8 us
    pallas_call x1, Pallas kernels, legendre(): pl.pallas_call(legendre_kernel, grid=(padded // SLOT_PAD,), out_shape=jax...  9.57 us
    unnamed x55, local copies, waits for them, and re-layouts  9.25 us
    mul x4, other arithmetic, advance_coupled_model(): east_flux = zonal_exchange_factor * (jnp.roll(centre, -1, axis=2) - centre)  4.59 us
    slice x7, local copies, waits for them, and re-layouts, advance_coupled_model(): east_flux = zonal_exchange_factor * (jnp.roll(centre, -1, axis=2) - centre)  4.56 us
    add x4, other arithmetic, advance_coupled_model(): return centre + meridional + zonal_div + vertical + forced  4.03 us
    slice x4, local copies, waits for them, and re-layouts, advance_coupled_model(): meridian_exchange_factor[1:] * (bordered_array[:, 2:] - centre)  2.92 us
  transfers between devices with their start and end apart: 4, of which 0 were waited for; matrix products, arithmetic and copies ran while one was open for 15% of the time, Pallas kernels for 7%

profile of v2, /device:TPU:0, one launch (start us, length us, event | category | flops | bytes accessed | tf_op | source)
XLA Modules:
  0.0 128.4 jit_solution(15999070856223080898)
XLA Ops:
  0.7 1.6 %sqrt_multiply_fusion = f32[1,1,5120]{2,1,0:T(1,128)} fusion(bf16[1,64,5120]{2,1,0:T(8,128)(2,1)} %param.10), kind=kLoop, calls=%fused_computation.129 | loop fusion | flops 35840 | bytes 40960 | tf_op jit(solution)/shard_map/mul | solution.py:421
  2.3 1.5 %slice_reduce_fusion = bf16[5120]{0:T(1024)(128)(2,1)} fusion(bf16[1,64,5120]{2,1,0:T(8,128)(2,1)} %param.10), kind=kLoop, calls=%fused_computation.130 | loop fusion | bytes 20480 | tf_op jit(solution)/shard_map/slice | solution.py:425
  6.4 3.4 %copy.12 = bf16[214,640,4]{0,1,2:T(8,128)(2,1)} copy(bf16[214,640,4]{1,2,0:T(4,128)(2,1)} %param.13) | data formatting | bytes 2191360 | tf_op args[3]
  9.8 2.0 %copy.13 = bf16[214,8,80,4]{2,0,3,1:T(8,128)(2,1)S(1)} copy(bf16[214,8,80,4]{0,2,1,3:T(8,128)(2,1)} %bitcast.52) | data formatting | bytes 2191360 | tf_op jit(solution)/shard_map/reshape | solution.py:390
  13.8 53.1 %shard_map.113 = (bf16[8,4,224,128]{3,2,1,0:T(8,128)(2,1)S(1)}, bf16[8,4,224,128]{3,2,1,0:T(8,128)(2,1)S(1)}, f32[8,4,4096]{2,1,0:T(4,128)S(1)}, f32[4,4096]{1,0...) custom-call(s32[1]{0:T(128)} %copy.15.points_ref, ...), custom_call_target="tpu_custom_call" | custom-call | flops 838860800 | bytes 8388608 | tf_op jit(solution)/shard_map/pallas_call | solution.py:235
  66.9 1.3 copy-done.1
  70.5 1.0 fusion.48
  73.2 0.9 fusion.11
  74.1 1.2 select_reduce_fusion
  76.0 1.3 collective-permute-start
  77.2 1.3 %collective-permute-start.1 = (f32[4096]{0:T(1024)}, f32[4096]{0:T(1024)}, u32[]{:S(2)}, u32[]{:S(2)}) collective-permute-start(f32[4096]{0:T(1024)} %bitcast.16), channel_id=1, source_target_pairs={{1,0},{2,1},{3,2},{4,3},{5,4},{6,5},{7,6},{8,7},{9,8},{10,9},{11,1... | collective-permute-start | bytes 49160 | tf_op jit(solution)/shard_map/ppermute | solution.py:327
  78.5 4.9 %collective-permute-start.2 = (f32[4096]{0:T(1024)}, f32[4096]{0:T(1024)}, u32[]{:S(2)}, u32[]{:S(2)}) collective-permute-start(f32[4096]{0:T(1024)} %bitcast.16), channel_id=1, source_target_pairs={{0,1},{1,2},{2,3},{3,4},{4,5},{5,6},{6,7},{7,8},{8,9},{9,10},{10,1... | collective-permute-start | bytes 49160 | tf_op jit(solution)/shard_map/ppermute | solution.py:327
  83.5 4.3 %collective-permute-start.3 = (f32[4096]{0:T(1024)}, f32[4096]{0:T(1024)}, u32[]{:S(2)}, u32[]{:S(2)}) collective-permute-start(f32[4096]{0:T(1024)} %bitcast.16), channel_id=1, source_target_pairs={{0,2},{1,3},{2,4},{3,5},{4,6},{5,7},{6,8},{7,9},{8,10},{9,11},{10,... | collective-permute-start | bytes 49160 | tf_op jit(solution)/shard_map/ppermute | solution.py:327
  87.8 1.7 %pad_maximum_fusion.2 = f32[8,12,4096]{2,1,0:T(8,128)} fusion(f32[8,4,4096]{2,1,0:T(4,128)S(1)} %get-tuple-element.52, f32[8,4,4096]{2,1,0:T(4,128)S(1)} %copy-done, f32[8,4,4096]{2,1,0:T(4,128)S(1)} %copy-done.10), kind=kLoop, calls=%fused_computation.16 | loop fusion | flops 786432 | bytes 3145728 | tf_op jit(solution)/shard_map/concatenate | solution.py:431
  89.6 0.8 slice.362
  91.2 0.8 slice.360
  96.5 1.2 fusion.47
  98.4 3.5 %slice.365 = f32[8,10,4095]{2,1,0:T(8,128)} slice(f32[8,12,4096]{2,1,0:T(8,128)} %pad_maximum_fusion.2), slice={[0:8], [1:11], [1:4096]} | slice | bytes 2620800 | tf_op jit(solution)/shard_map/jit(_roll_static)/slice | solution.py:341
  102.6 4.0 %fusion.2 = f32[8,10,4096]{2,1,0:T(8,128)} fusion(f32[8,4,4096]{2,1,0:T(4,128)S(1)} %get-tuple-element.52, f32[8,4,4096]{2,1,0:T(4,128)S(1)} %copy-done, f32[8,4,4096]{2,1,0:T(4,128)} %copy-done.9, f32[8,10,4095]{2,1,0:T(8,128)} %slice.365, f32[8,12,4096]{2,1,0:T(8,128)} %pad_maximum_fusion.2, f32[10,4096]{1,0:T(8,128)} %slice.364), kind=kLoop, calls=%fused_computation.5 | loop fusion | flops 1638400 | bytes 5668544 | tf_op jit(solution)/shard_map/mul | solution.py:341
  106.6 1.5 %copy-done.2 = bf16[8,4,224,128]{3,2,1,0:T(8,128)(2,1)S(1)} copy-done((bf16[8,4,224,128]{3,2,1,0:T(8,128)(2,1)S(1)}, bf16[8,4,224,128]{3,2,1,0:T(8,128)(2,1)}, u32[]{:S(2)}) %copy-start.2) | copy-done | bytes 1835032
  108.2 9.6 %shard_map.114 = f32[214,80,128]{2,1,0:T(8,128)} custom-call(s32[1]{0:T(128)} %bitcast.degree_ref, s32[224]{0:T(256)S(1)} %dynamic_slice.3.slots_ref, bf16[32,224,128]{2,1,0:T(8,128)(2,1)S(1)} %bitcast.45, bf16[32,224,128]{2,1,0:T(8,128)(2,1)S(1)} %bitcast.44), custom_call_target="tpu_custom_call" | custom-call | flops 1174405120 | bytes 12435456 | tf_op jit(solution)/shard_map/pallas_call | solution.py:290
  118.0 1.1 maximum_multiply_fusion.1
  120.4 1.4 %fusion.8 = f32[8,10,4096]{2,1,0:T(8,128)S(1)} fusion(f32[8,12,4096]{2,1,0:T(8,128)S(1)} %copy-done.7, f32[8,10,4096]{2,1,0:T(8,128)S(1)} %copy-done.8, f32[8,10,4095]{2,1,0:T(8,128)S(1)} %bitcast.47, f32[8,10,1]{2,1,0:T(8,128)S(1)} %slice.366, f32[1,10,4096]{2,1,0:T(8,128)S(1)} %slice_bitcast_fusion, f32[7,10,4096]{2,1,0:T(8,128)S(1)} %fusion.10, ...), kind=kLoop, calls=%fused_computation.13 | loop fusion | flops 3932160 | bytes 9502720 | tf_op jit(solution)/shard_map/add | solution.py:349
  127.0 1.4 %fusion.37 = f32[8,4,4096]{2,1,0:T(4,128)} fusion(f32[8,6,4096]{2,1,0:T(8,128)S(1)} %fusion.17, f32[8,4,4096]{2,1,0:T(4,128)S(1)} %fusion.39, f32[8,4,4095]{2,1,0:T(4,128)S(1)} %bitcast.53, f32[8,4,1]{2,1,0:T(4,128)S(1)} %slice.415, f32[1,4,4096]{2,1,0:T(4,128)S(1)} %slice_bitcast_fusion.3, f32[7,4,4096]{2,1,0:T(4,128)S(1)} %fusion.42, ...), kind=kLoop, calls=%fused_computation.59 | loop fusion | flops 1572864 | bytes 3801088 | tf_op jit(solution)/shard_map/add | solution.py:349
  (133 shorter events, 20.9 us)
Async XLA Ops:
  9.8 2.0 %copy-start = (f32[8,4,4096]{2,1,0:T(4,128)S(1)}, f32[8,4,4096]{2,1,0:T(4,128)}, u32[]{:S(2)}) copy-start(f32[8,4,4096]{2,1,0:T(4,128)} %refs_0_.1) | copy-start | bytes 1572868
  12.7 1.1 copy-start.4
  12.7 1.1 copy-start.5
  12.7 1.1 copy-start.6
  66.9 1.3 copy-start.1
  71.8 2.3 %copy-start.24 = (bf16[5120]{0:T(1024)(128)(2,1)S(1)}, bf16[5120]{0:T(1024)(128)(2,1)}, u32[]{:S(2)}) copy-start(bf16[5120]{0:T(1024)(128)(2,1)} %slice_reduce_fusion) | copy-start | bytes 30724
  74.1 13.7 %copy-start.10 = (f32[8,4,4096]{2,1,0:T(4,128)S(1)}, f32[8,4,4096]{2,1,0:T(4,128)}, u32[]{:S(2)}) copy-start(f32[8,4,4096]{2,1,0:T(4,128)} %copy-done.9) | copy-start | bytes 1572868
  76.0 41.9 %collective-permute-start = (f32[4096]{0:T(1024)}, f32[4096]{0:T(1024)}, u32[]{:S(2)}, u32[]{:S(2)}) collective-permute-start(f32[4096]{0:T(1024)} %bitcast.16), channel_id=1, source_target_pairs={{2,0},{3,1},{4,2},{5,3},{6,4},{7,5},{8,6},{9,7},{10,8},{11,9},{12,... | collective-permute-start | bytes 49160 | tf_op jit(solution)/shard_map/ppermute | solution.py:327
  77.2 40.7 %collective-permute-start.1 = (f32[4096]{0:T(1024)}, f32[4096]{0:T(1024)}, u32[]{:S(2)}, u32[]{:S(2)}) collective-permute-start(f32[4096]{0:T(1024)} %bitcast.16), channel_id=1, source_target_pairs={{1,0},{2,1},{3,2},{4,3},{5,4},{6,5},{7,6},{8,7},{9,8},{10,9},{11,1... | collective-permute-start | bytes 49160 | tf_op jit(solution)/shard_map/ppermute | solution.py:327
  78.5 39.4 %collective-permute-start.2 = (f32[4096]{0:T(1024)}, f32[4096]{0:T(1024)}, u32[]{:S(2)}, u32[]{:S(2)}) collective-permute-start(f32[4096]{0:T(1024)} %bitcast.16), channel_id=1, source_target_pairs={{0,1},{1,2},{2,3},{3,4},{4,5},{5,6},{6,7},{7,8},{8,9},{9,10},{10,1... | collective-permute-start | bytes 49160 | tf_op jit(solution)/shard_map/ppermute | solution.py:327
  83.5 34.4 %collective-permute-start.3 = (f32[4096]{0:T(1024)}, f32[4096]{0:T(1024)}, u32[]{:S(2)}, u32[]{:S(2)}) collective-permute-start(f32[4096]{0:T(1024)} %bitcast.16), channel_id=1, source_target_pairs={{0,2},{1,3},{2,4},{3,5},{4,6},{5,7},{6,8},{7,9},{8,10},{9,11},{10,... | collective-permute-start | bytes 49160 | tf_op jit(solution)/shard_map/ppermute | solution.py:327
  89.5 1.6 %copy-start.11 = (s32[4,4096]{1,0:T(4,128)}, s32[4,4096]{1,0:T(4,128)S(1)}, u32[]{:S(2)}) copy-start(s32[4,4096]{1,0:T(4,128)S(1)} %get-tuple-element.55) | copy-start | bytes 196612
  91.0 3.9 %copy-start.15 = (f32[4,4096]{1,0:T(4,128)}, f32[4,4096]{1,0:T(4,128)S(1)}, u32[]{:S(2)}) copy-start(f32[4,4096]{1,0:T(4,128)S(1)} %get-tuple-element.58) | copy-start | bytes 196612
  91.0 3.9 %copy-start.16 = (f32[4,4096]{1,0:T(4,128)}, f32[4,4096]{1,0:T(4,128)S(1)}, u32[]{:S(2)}) copy-start(f32[4,4096]{1,0:T(4,128)S(1)} %get-tuple-element.59) | copy-start | bytes 196612
  106.6 1.5 %copy-start.2 = (bf16[8,4,224,128]{3,2,1,0:T(8,128)(2,1)S(1)}, bf16[8,4,224,128]{3,2,1,0:T(8,128)(2,1)}, u32[]{:S(2)}) copy-start(bf16[8,4,224,128]{3,2,1,0:T(8,128)(2,1)} %copy-done.1) | copy-start | bytes 5505028
  108.1 9.7 %copy-start.8 = (f32[8,10,4096]{2,1,0:T(8,128)S(1)}, f32[8,10,4096]{2,1,0:T(8,128)}, u32[]{:S(2)}) copy-start(f32[8,10,4096]{2,1,0:T(8,128)} %fusion.2) | copy-start | bytes 3932164
  108.1 9.8 %copy-start.12 = (s32[4,4096]{1,0:T(4,128)S(1)}, s32[4,4096]{1,0:T(4,128)}, u32[]{:S(2)}) copy-start(s32[4,4096]{1,0:T(4,128)} %copy-done.11) | copy-start | bytes 196612
  108.1 9.8 %copy-start.21 = (f32[4,4096]{1,0:T(4,128)S(1)}, f32[4,4096]{1,0:T(4,128)}, u32[]{:S(2)}) copy-start(f32[4,4096]{1,0:T(4,128)} %get-tuple-element.57) | copy-start | bytes 196612
  108.1 9.8 %copy-start.25 = (pred[12]{0:T(512)(128)(4,1)S(1)}, pred[12]{0:T(512)(128)(4,1)}, u32[]{:S(2)}) copy-start(pred[12]{0:T(512)(128)(4,1)} %get-tuple-element.44) | copy-start | bytes 40
  108.1 9.8 %copy-start.26 = (pred[12]{0:T(512)(128)(4,1)S(1)}, pred[12]{0:T(512)(128)(4,1)}, u32[]{:S(2)}) copy-start(pred[12]{0:T(512)(128)(4,1)} %get-tuple-element.45) | copy-start | bytes 40
  117.7 1.7 %copy-start.7 = (f32[8,12,4096]{2,1,0:T(8,128)S(1)}, f32[8,12,4096]{2,1,0:T(8,128)}, u32[]{:S(2)}) copy-start(f32[8,12,4096]{2,1,0:T(8,128)} %pad_maximum_fusion.2) | copy-start | bytes 4718596
  119.4 1.0 copy-start.14
  122.5 1.0 copy-start.20
  124.6 1.0 copy-start.18
  (7 other events, 6.2 us)

commit v3 on v2

--- a/solution.py
+++ b/solution.py
@@ -54,11 +54,9 @@
     *refs,
 ):
     sec_count, lat_count, col_count = sizes
-    halo = refs[:5]
-    coef_out, weight_out = refs[5:7]
-    before, after = refs[7:12], refs[12:17]
+    halo, coef_out, weight_out, before, after = refs[:5]
     (base_ref, acc_ref, mine_ref, local_sem, weight_send, weight_recv, halo_send, halo_recv,
-     lat_send, lat_recv, group_send, group_recv) = refs[17:]
+     lat_send, lat_recv, sec_send, sec_recv, col_send, col_recv) = refs[5:]
     groups = sec_count * col_count
     devices = groups * lat_count
     sec, lat, col = (lax.axis_index(name) for name in LINE)
@@ -100,19 +98,17 @@
             device_id_type=MESH,
         )
 
-    def halo_copies():
-        return [
-            pltpu.make_async_remote_copy(
-                src_ref=halo[k],
-                dst_ref=target[k],
-                send_sem=halo_send.at[side, k],
-                recv_sem=halo_recv.at[side, k],
-                device_id=place,
-                device_id_type=MESH,
-            )
-            for k in range(5)
-            for side, (target, place) in enumerate(((before, following), (after, previous)))
-        ]
+    def halo_copy(side):
+        return pltpu.make_async_remote_copy(
+            src_ref=halo,
+            dst_ref=(before, after)[side],
+            send_sem=halo_send.at[side],
+            recv_sem=halo_recv.at[side],
+            device_id=(following, previous)[side],
+            device_id_type=MESH,
+        )
+
+    has_next, has_previous = line < devices - 1, line > 0
 
     def lat_copy(step):
         other, place = lat_place(step)
@@ -125,24 +121,41 @@
             device_id_type=MESH,
         )
 
-    def group_copy(step):
+    def sec_copy(step):
         return pltpu.make_async_remote_copy(
             src_ref=coef_out.at[group],
             dst_ref=coef_out.at[group],
-            send_sem=group_send.at[step],
-            recv_sem=group_recv.at[step],
-            device_id=group_place(step)[1],
+            send_sem=sec_send.at[step],
+            recv_sem=sec_recv.at[step],
+            device_id={"sec": (sec + step) % sec_count, "lat": lat, "col": col},
             device_id_type=MESH,
         )
 
-    for copy in halo_copies():
-        copy.start()
+    def col_copy(back, step):
+        block = (sec + sec_count - back) % sec_count * col_count + col
+        return pltpu.make_async_remote_copy(
+            src_ref=coef_out.at[block],
+            dst_ref=coef_out.at[block],
+            send_sem=col_send.at[back, step],
+            recv_sem=col_recv.at[back, step],
+            device_id={"sec": sec, "lat": lat, "col": (col + step) % col_count},
+            device_id_type=MESH,
+        )
+
     own_weights = pltpu.make_async_copy(weight_ref.at[group], weight_out.at[group], local_sem.at[0])
     own_weights.start()
 
     @pl.loop(1, groups)
     def _(step):
         weight_copy(step).start()
+
+    @pl.when(has_next)
+    def _():
+        halo_copy(0).start()
+
+    @pl.when(has_previous)
+    def _():
+        halo_copy(1).start()
 
     points = points_ref[0]
     waves = table_ref.shape[2]
@@ -202,25 +215,51 @@
     def _(step):
         lat_copy(step).wait_recv()
 
+    @pl.loop(1, sec_count)
+    def _(step):
+        sec_copy(step).start()
+
+    @pl.loop(1, col_count)
+    def _(step):
+        col_copy(0, step).start()
+
+    @pl.loop(1, sec_count)
+    def _(back):
+        sec_copy(back).wait_recv()
+
+        @pl.loop(1, col_count)
+        def _(step):
+            col_copy(back, step).start()
+
+    @pl.when(has_next)
+    def _():
+        halo_copy(0).wait_send()
+        halo_copy(1).wait_recv()
+
+    @pl.when(has_previous)
+    def _():
+        halo_copy(1).wait_send()
+        halo_copy(0).wait_recv()
+
+    own_weights.wait()
+
     @pl.loop(1, groups)
     def _(step):
-        group_copy(step).start()
-
-    for copy in halo_copies():
-        copy.wait()
-    own_weights.wait()
-
-    @pl.loop(1, groups)
-    def _(step):
         weight_copy(step).wait()
 
     @pl.loop(1, lat_count)
     def _(step):
         lat_copy(step).wait_send()
 
-    @pl.loop(1, groups)
-    def _(step):
-        group_copy(step).wait()
+    @pl.loop(1, sec_count)
+    def _(step):
+        sec_copy(step).wait_send()
+
+    @pl.loop(0, sec_count)
+    def _(back):
+        @pl.loop(1, col_count)
+        def _(step):
+            col_copy(back, step).wait()
 
 
 def exchange(sizes, points, table, slots, state, weights, halo):
@@ -228,21 +267,20 @@
     waves = table.shape[2]
     sec_count, lat_count, col_count = sizes
     groups = sec_count * col_count
-    padded = weights.shape[2]
+    padded = weights.shape[1]
     anywhere = pl.BlockSpec(memory_space=pl.ANY)
     inside = pl.BlockSpec(memory_space=pltpu.VMEM)
-    halo_shapes = [jax.ShapeDtypeStruct(part.shape, part.dtype) for part in halo]
+    halo_shape = jax.ShapeDtypeStruct(halo.shape, halo.dtype)
     out = pl.pallas_call(
         functools.partial(exchange_kernel, sizes),
         out_shape=[
             jax.ShapeDtypeStruct((groups, lat_count, padded, 2 * fields), jnp.bfloat16),
             jax.ShapeDtypeStruct(weights.shape, jnp.bfloat16),
-        ]
-        + halo_shapes
-        + halo_shapes,
-        in_specs=[pl.BlockSpec(memory_space=pltpu.SMEM), inside, inside, inside, anywhere]
-        + [anywhere] * 5,
-        out_specs=[anywhere] * 12,
+            halo_shape,
+            halo_shape,
+        ],
+        in_specs=[pl.BlockSpec(memory_space=pltpu.SMEM), inside, inside, inside, anywhere, anywhere],
+        out_specs=[anywhere] * 4,
         scratch_shapes=[
             pltpu.VMEM((2, CHUNK, waves), jnp.float32),
             pltpu.VMEM((2 * fields, waves), jnp.float32),
@@ -250,12 +288,14 @@
             pltpu.SemaphoreType.DMA((2,)),
             pltpu.SemaphoreType.DMA((groups,)),
             pltpu.SemaphoreType.DMA((groups,)),
-            pltpu.SemaphoreType.DMA((2, 5)),
-            pltpu.SemaphoreType.DMA((2, 5)),
+            pltpu.SemaphoreType.DMA((2,)),
+            pltpu.SemaphoreType.DMA((2,)),
             pltpu.SemaphoreType.DMA((lat_count,)),
             pltpu.SemaphoreType.DMA((lat_count,)),
-            pltpu.SemaphoreType.DMA((groups,)),
-            pltpu.SemaphoreType.DMA((groups,)),
+            pltpu.SemaphoreType.DMA((sec_count,)),
+            pltpu.SemaphoreType.DMA((sec_count,)),
+            pltpu.SemaphoreType.DMA((sec_count, col_count)),
+            pltpu.SemaphoreType.DMA((sec_count, col_count)),
         ],
         compiler_params=pltpu.CompilerParams(
             vmem_limit_bytes=24 * 2**20, collective_id=0, has_side_effects=True
@@ -263,20 +303,32 @@
         cost_estimate=pl.CostEstimate(
             flops=4 * fields * waves * width, bytes_accessed=8 * 2**20, transcendentals=0
         ),
-    )(points, table, slots, state, weights, *halo)
-    return out[0], out[1], out[2:7], out[7:12]
+    )(points, table, slots, state, weights, halo)
+    return out
 
 
 def legendre_kernel(degree_ref, slots_ref, weight_ref, coef_ref, out_ref):
-    rows, pair, width = coef_ref.shape
+    groups, lines, pair, width = coef_ref.shape
+    rows = groups * lines
+    packed = weight_ref.shape[2]
     degrees = out_ref.shape[1]
     first = degree_ref[0]
     for half in range(pair // 8):
         cut = slice(half * 8, half * 8 + 8)
-        values = weight_ref[:, cut, :].astype(jnp.float32).reshape(rows * 8, weight_ref.shape[2])
-        values = values.T[:degrees]
+        held = weight_ref[:, cut, :].astype(jnp.float32).reshape(groups * 8, packed)
+        parts = [
+            pltpu.roll(held, (packed - q * degrees) % packed, 1)[:, :128] if q else held[:, :128]
+            for q in range(lines)
+        ]
+        values = jnp.concatenate(parts, axis=0).T[:degrees]
         lane_slot = lax.broadcasted_iota(jnp.int32, (degrees, rows * 8), 1) % 8
-        coefs = coef_ref[:, cut, :].astype(jnp.float32).reshape(rows * 8, width).astype(jnp.bfloat16)
+        coefs = jnp.concatenate(
+            [
+                coef_ref[:, q, cut, :].astype(jnp.float32).reshape(groups * 8, width)
+                for q in range(lines)
+            ],
+            axis=0,
+        ).astype(jnp.bfloat16)
         degree = first + lax.broadcasted_iota(jnp.int32, (degrees, width), 0)
         for s in range(8):
             wave = slots_ref[pl.program_id(0) * pair + half * 8 + s]
@@ -286,7 +338,8 @@
 
 
 def legendre(weights, coefs, slots, first_degree, slot_count, degrees):
-    rows, padded, width = coefs.shape
+    groups, lines, padded, width = coefs.shape
+    rows = groups * lines
     return pl.pallas_call(
         legendre_kernel,
         grid=(padded // SLOT_PAD,),
@@ -294,11 +347,11 @@
         in_specs=[
             pl.BlockSpec(memory_space=pltpu.SMEM),
             pl.BlockSpec(memory_space=pltpu.SMEM),
-            pl.BlockSpec((rows, SLOT_PAD, weights.shape[2]), lambda i: (0, i, 0)),
-            pl.BlockSpec((rows, SLOT_PAD, width), lambda i: (0, i, 0)),
+            pl.BlockSpec((groups, SLOT_PAD, weights.shape[2]), lambda i: (0, i, 0)),
+            pl.BlockSpec((groups, lines, SLOT_PAD, width), lambda i: (0, 0, i, 0)),
         ],
         out_specs=pl.BlockSpec((SLOT_PAD, degrees, width), lambda i: (i, 0, 0)),
-        compiler_params=pltpu.CompilerParams(vmem_limit_bytes=40 * 2**20),
+        compiler_params=pltpu.CompilerParams(vmem_limit_bytes=(8 if rows <= 64 else 32) * 2**20),
         cost_estimate=pl.CostEstimate(
             flops=2 * rows * padded * width * degrees * 8,
             bytes_accessed=4 * slot_count * degrees * width + 4 * rows * padded * width,
@@ -379,17 +432,22 @@
     span = marine_tracer_state.shape[2]
     layers = marine_tracer_state.shape[0]
     relative = overlying_parallel - linear_index
-    halo = [
-        marine_tracer_state,
-        lateral_diffusivity,
-        depthwise_diffusivity,
-        water_indicator,
-        jnp.broadcast_to(jnp.tile(relative, 2)[:, None], (2 * rows, 128)),
-    ]
+    payload = jnp.concatenate(
+        [
+            marine_tracer_state,
+            lateral_diffusivity[None],
+            depthwise_diffusivity[None],
+            water_indicator.astype(jnp.float32)[None],
+            jnp.broadcast_to(relative.astype(jnp.float32)[:, None], (rows, span))[None],
+        ],
+        axis=0,
+    )
+    halo = payload.astype(jnp.bfloat16).reshape((layers + 4) * rows, span)
 
     send = weighted_associated_polynomials.reshape(slot_count, groups, block_degrees, row_count)
-    send = jnp.transpose(send, (1, 3, 0, 2))
-    send = jnp.pad(send, ((0, 0), (0, 0), (0, padded - slot_count), (0, 128 - block_degrees)))
+    send = jnp.transpose(send, (1, 0, 3, 2)).reshape(groups, slot_count, row_count * block_degrees)
+    lanes = -(-send.shape[2] // 128) * 128
+    send = jnp.pad(send, ((0, 0), (0, padded - slot_count), (0, lanes - send.shape[2])))
     slots = zonal_mode_assignment.reshape(lat_count, slot_count)
     slots = jnp.pad(slots, ((0, 0), (0, padded - slot_count)), constant_values=wave_count)
     coefs, weights, before, after = exchange(
@@ -401,13 +459,13 @@
         send,
         halo,
     )
-    coefs = coefs.reshape(groups * lat_count, padded, coefs.shape[3])
-    weights = weights.reshape(groups * row_count, padded, 128)
     first, last = linear_index == 0, linear_index == devices - 1
-    before = [jnp.where(first, jnp.zeros_like(part), part) for part in before]
-    after = [jnp.where(last, jnp.zeros_like(part), part) for part in after]
-
-    surface = jnp.concatenate([before[0][0], marine_tracer_state[0], after[0][0]], axis=0)
+    before = jnp.where(first, jnp.zeros_like(before), before).astype(jnp.float32)
+    after = jnp.where(last, jnp.zeros_like(after), after).astype(jnp.float32)
+    before = before.reshape(payload.shape)
+    after = after.reshape(payload.shape)
+
+    surface = jnp.concatenate([before[0], marine_tracer_state[0], after[0]], axis=0)
     under = underlying_marine_parallel[0] - (linear_index - 1) * rows
     skin = jnp.where(jnp.arange(3 * rows)[:, None] == under, surface, 0.0).sum(axis=0)
     ocean_points = jnp.arange(span, dtype=jnp.int32)
@@ -428,14 +486,11 @@
         step: shifted(flux, LINE, devices, -step) if step else flux for step in (-2, -1, 0, 1, 2)
     }
 
-    thermal = jnp.concatenate([before[0], marine_tracer_state, after[0]], axis=1)
-    kappa, depth, sea = (
-        jnp.concatenate([before[k], halo[k], after[k]], axis=0) for k in (1, 2, 3)
-    )
-    sea = sea.astype(jnp.float32)
-    relative = jnp.concatenate([before[4][:rows, :1], relative[:, None], after[4][:rows, :1]], axis=0)
+    whole = jnp.concatenate([before, payload, after], axis=1)
+    thermal = whole[:layers]
+    kappa, depth, sea, relative = (whole[layers + k] for k in range(4))
     owner = jnp.arange(3 * rows, dtype=jnp.int32)[:, None] // rows - 1
-    target = relative + owner
+    target = relative + owner.astype(jnp.float32)
     forcing = jnp.zeros_like(sea)
     for step, row in flux_near.items():
         forcing = jnp.where(target == step, row[None], forcing)

time: 131 us -> 108 us (0.82)
  the two profiles are of different devices: /device:TPU:0 before, /device:TPU:27 now
where the time goes in v3:
time: 108 us; the launch traced here: 107 us
  Pallas kernels  45.5 us (42%)
  local copies, waits for them, and re-layouts  28.6 us (26%)
  starting transfers between devices  14.6 us (14%)
  other arithmetic  13.9 us (13%)
  between operations  2.69 us (2%)
  matrix products  2.11 us (2%)
    pallas_call x1, Pallas kernels, exchange(): pl.pallas_call(functools.partial(exchange_kernel, sizes), out_shape=[jax....  35.3 us
    ppermute x4, starting transfers between devices, shifted(): return lax.ppermute(array, axis, pairs)  14.6 us
    unnamed x48, local copies, waits for them, and re-layouts  11.5 us
    pallas_call x1, Pallas kernels, legendre(): pl.pallas_call(legendre_kernel, grid=(padded // SLOT_PAD,), out_shape=jax...  10.2 us
    add x4, other arithmetic, advance_coupled_model(): return centre + meridional + zonal_div + vertical + forced  4.07 us
    slice x4, local copies, waits for them, and re-layouts, advance_coupled_model(): meridian_exchange_factor[1:] * (bordered_array[:, 2:] - centre)  2.82 us
    reshape x1, local copies, waits for them, and re-layouts, body(): after = after.reshape(payload.shape)  2.52 us
    transpose x1, local copies, waits for them, and re-layouts, body(): jnp.transpose(send, (1, 0, 3, 2))  2.5 us
  transfers between devices with their start and end apart: 4, of which 0 were waited for; matrix products, arithmetic and copies ran while one was open for 10% of the time, Pallas kernels for 9%

profile of v3, /device:TPU:27, one launch (start us, length us, event | category | flops | bytes accessed | tf_op | source)
XLA Modules:
  0.0 107.4 jit_solution(10330130076503648696)
XLA Ops:
  0.7 1.1 %constant_dynamic-update-slice_fusion = f32[12,4,4096]{2,1,0:T(4,128)S(1)} fusion(f32[8,4,4096]{2,1,0:T(4,128)} %param.14), kind=kLoop, calls=%fused_computation.159 | loop fusion | bytes 1048576
  2.6 1.0 sqrt_multiply_fusion
  3.6 1.0 slice_reduce_fusion
  7.7 0.9 bitcast_dynamic-update-slice_fusion
  9.4 3.4 %copy.13 = bf16[214,640,4]{0,1,2:T(8,128)(2,1)} copy(bf16[214,640,4]{1,2,0:T(4,128)(2,1)} %param.13) | data formatting | bytes 2191360 | tf_op args[3]
  12.8 2.5 %copy.14 = bf16[8,214,4,80]{1,3,2,0:T(8,128)(2,1)} copy(bf16[8,214,4,80]{1,3,0,2:T(8,128)(2,1)} %bitcast.90) | data formatting | bytes 2191360 | tf_op jit(solution)/shard_map/transpose | solution.py:448
  15.3 1.8 %copy.15 = bf16[8,214,320]{2,1,0:T(8,128)(2,1)S(1)} copy(bf16[8,214,320]{1,2,0:T(8,128)(2,1)} %bitcast.89) | data formatting | bytes 2191360 | tf_op jit(solution)/shard_map/reshape | solution.py:448
  18.2 35.3 %shard_map.113 = (bf16[8,4,224,128]{3,2,1,0:T(8,128)(2,1)S(1)}, bf16[8,224,384]{2,1,0:T(8,128)(2,1)S(1)}, bf16[48,4096]{1,0:T(8,128)(2,1)S(1)}, bf16[48,4096]{1,0:T(8,128)(2,1)S(1)}) custom-call(s32[1]{0:T(128)} %copy.21.points_ref, f32[2,60,640]{2,1,0:T(8,128)S(1)} %maximum_multiply_fusion.table_ref, s32[896,1]{1,0:T(8,128)S(1)} %reshape.495.slots_ref, ...), custom_call_target="tpu_custom_call" | custom-call | flops 838860800 | bytes 8388608 | tf_op jit(solution)/shard_map/pallas_call | solution.py:274
  53.5 1.1 copy-done
  54.7 0.9 copy-done.12
  57.5 0.9 fusion.11
  58.4 1.2 %select_reduce_fusion = f32[3,4096]{1,0:T(4,128)S(1)} fusion(pred[128,4096]{1,0:T(8,128)(4,1)S(1)} %iota_compare_fusion.1, s32[4096]{0:T(1024)S(1)} %get-tuple-element.31, bf16[1,40,128]{2,1,0:T(8,128)(2,1)S(1)} %bitcast.93, bf16[1,40,128]{2,1,0:T(8,128)(2,1)S(1)} %get-tuple-element.24, bf16[1,40,128]{2,1,0:T(8,128)(2,1)S(1)} %get-tuple-element.23), kind=kOutput, calls=%fused_computation | convolution fusion | flops 129157120 | bytes 620544 | tf_op jit(solution)/shard_map/kta,tx->kax/dot_general | solution.py:373
  60.3 1.9 %collective-permute-start = (f32[4096]{0:T(1024)}, f32[4096]{0:T(1024)}, u32[]{:S(2)}, u32[]{:S(2)}) collective-permute-start(f32[4096]{0:T(1024)} %bitcast.22), channel_id=1, source_target_pairs={{2,0},{3,1},{4,2},{5,3},{6,4},{7,5},{8,6},{9,7},{10,8},{11,9},{12,... | collective-permute-start | bytes 49160 | tf_op jit(solution)/shard_map/ppermute | solution.py:380
  62.2 2.1 %collective-permute-start.1 = (f32[4096]{0:T(1024)}, f32[4096]{0:T(1024)}, u32[]{:S(2)}, u32[]{:S(2)}) collective-permute-start(f32[4096]{0:T(1024)} %bitcast.22), channel_id=1, source_target_pairs={{1,0},{2,1},{3,2},{4,3},{5,4},{6,5},{7,6},{8,7},{9,8},{10,9},{11,1... | collective-permute-start | bytes 49160 | tf_op jit(solution)/shard_map/ppermute | solution.py:380
  64.3 7.2 %collective-permute-start.2 = (f32[4096]{0:T(1024)}, f32[4096]{0:T(1024)}, u32[]{:S(2)}, u32[]{:S(2)}) collective-permute-start(f32[4096]{0:T(1024)} %bitcast.22), channel_id=1, source_target_pairs={{0,1},{1,2},{2,3},{3,4},{4,5},{5,6},{6,7},{7,8},{8,9},{9,10},{10,1... | collective-permute-start | bytes 49160 | tf_op jit(solution)/shard_map/ppermute | solution.py:380
  71.4 3.5 %collective-permute-start.3 = (f32[4096]{0:T(1024)}, f32[4096]{0:T(1024)}, u32[]{:S(2)}, u32[]{:S(2)}) collective-permute-start(f32[4096]{0:T(1024)} %bitcast.22), channel_id=1, source_target_pairs={{0,2},{1,3},{2,4},{3,5},{4,6},{5,7},{6,8},{7,9},{8,10},{9,11},{10,... | collective-permute-start | bytes 49160 | tf_op jit(solution)/shard_map/ppermute | solution.py:380
  74.9 1.4 %reshape.488 = f32[12,4,4096]{2,1,0:T(4,128)S(1)} reshape(f32[48,4096]{1,0:T(8,128)} %copy-done.12) | data formatting | bytes 1572864 | tf_op jit(solution)/shard_map/reshape | solution.py:465
  76.3 2.5 %reshape.489 = f32[12,4,4096]{2,1,0:T(4,128)} reshape(f32[48,4096]{1,0:T(8,128)} %copy-done.11) | data formatting | bytes 1572864 | tf_op jit(solution)/shard_map/reshape | solution.py:466
  78.8 1.7 %pad_maximum_fusion = f32[12,12,4096]{2,1,0:T(8,128)S(1)} fusion(f32[12,4,4096]{2,1,0:T(4,128)} %reshape.489, f32[12,4,4096]{2,1,0:T(4,128)S(1)} %copy-done.6, f32[12,4,4096]{2,1,0:T(4,128)S(1)} %reshape.488), kind=kLoop, calls=%fused_computation.2 | loop fusion | flops 1179648 | bytes 4718592 | tf_op jit(solution)/shard_map/concatenate | solution.py:489
  80.5 0.9 slice_bitcast_fusion.3
  84.5 10.2 %shard_map.114 = f32[214,80,128]{2,1,0:T(8,128)} custom-call(s32[1]{0:T(128)} %bitcast.degree_ref, s32[224]{0:T(256)S(1)} %dynamic_slice.3.slots_ref, bf16[8,224,384]{2,1,0:T(8,128)(2,1)S(1)} %copy-done.1, bf16[8,4,224,128]{3,2,1,0:T(8,128)(2,1)S(1)} %get-tuple-element.7.coef_ref), custom_call_target="tpu_custom_call" | custom-call | flops 1174405120 | bytes 12435456 | tf_op jit(solution)/shard_map/pallas_call | solution.py:343
  95.7 1.0 fusion.45
  99.3 1.5 %fusion.8 = f32[8,10,4096]{2,1,0:T(8,128)S(1)} fusion(f32[12,12,4096]{2,1,0:T(8,128)S(1)} %copy-done.4, f32[8,10,4096]{2,1,0:T(8,128)S(1)} %fusion.2, f32[8,10,4095]{2,1,0:T(8,128)S(1)} %bitcast.85, f32[8,10,1]{2,1,0:T(8,128)S(1)} %slice.422, f32[1,10,4096]{2,1,0:T(8,128)S(1)} %slice_bitcast_fusion, f32[7,10,4096]{2,1,0:T(8,128)S(1)} %fusion.10, ...), kind=kLoop, calls=%fused_computation.14 | loop fusion | flops 3932160 | bytes 9502720 | tf_op jit(solution)/shard_map/add | solution.py:402
  106.0 1.4 %fusion.37 = f32[8,4,4096]{2,1,0:T(4,128)} fusion(f32[8,6,4096]{2,1,0:T(8,128)S(1)} %fusion.17, f32[8,4,4096]{2,1,0:T(4,128)S(1)} %fusion.39, f32[8,4,4095]{2,1,0:T(4,128)S(1)} %bitcast.91, f32[8,4,1]{2,1,0:T(4,128)S(1)} %slice.473, f32[1,4,4096]{2,1,0:T(4,128)S(1)} %slice_bitcast_fusion.13, f32[7,4,4096]{2,1,0:T(4,128)S(1)} %fusion.42, ...), kind=kLoop, calls=%fused_computation.59 | loop fusion | flops 1572864 | bytes 3801088 | tf_op jit(solution)/shard_map/add | solution.py:402
  (121 shorter events, 18.5 us)
Async XLA Ops:
  0.6 8.3 %copy-start.21 = (s32[856]{0:T(1024)S(1)}, s32[856]{0:T(1024)}, u32[]{:S(2)}) copy-start(s32[856]{0:T(1024)} %param.12) | copy-start | bytes 10276
  8.7 4.1 %copy-start.5 = (f32[12,4,4096]{2,1,0:T(4,128)}, f32[12,4,4096]{2,1,0:T(4,128)S(1)}, u32[]{:S(2)}) copy-start(f32[12,4,4096]{2,1,0:T(4,128)S(1)} %broadcast_dynamic-update-slice_fusion) | copy-start | bytes 2359300
  17.1 1.1 %copy-start.2 = (bf16[1,64,5120]{2,1,0:T(8,128)(2,1)S(1)}, bf16[1,64,5120]{2,1,0:T(8,128)(2,1)}, u32[]{:S(2)}) copy-start(bf16[1,64,5120]{2,1,0:T(8,128)(2,1)} %param.10) | copy-start | bytes 1966084
  53.5 1.1 %copy-start = (bf16[8,224,384]{2,1,0:T(8,128)(2,1)}, bf16[8,224,384]{2,1,0:T(8,128)(2,1)S(1)}, u32[]{:S(2)}) copy-start(bf16[8,224,384]{2,1,0:T(8,128)(2,1)S(1)} %get-tuple-element.6.weight_ref) | copy-start | bytes 4128772
  54.7 0.9 copy-start.12
  54.7 1.1 %copy-start.11 = (f32[48,4096]{1,0:T(8,128)}, f32[48,4096]{1,0:T(8,128)S(1)}, u32[]{:S(2)}) copy-start(f32[48,4096]{1,0:T(8,128)S(1)} %get-tuple-element.33) | copy-start | bytes 2359300
  59.6 19.2 %copy-start.6 = (f32[12,4,4096]{2,1,0:T(4,128)S(1)}, f32[12,4,4096]{2,1,0:T(4,128)}, u32[]{:S(2)}) copy-start(f32[12,4,4096]{2,1,0:T(4,128)} %copy-done.5) | copy-start | bytes 2359300
  60.3 35.4 %collective-permute-start = (f32[4096]{0:T(1024)}, f32[4096]{0:T(1024)}, u32[]{:S(2)}, u32[]{:S(2)}) collective-permute-start(f32[4096]{0:T(1024)} %bitcast.22), channel_id=1, source_target_pairs={{2,0},{3,1},{4,2},{5,3},{6,4},{7,5},{8,6},{9,7},{10,8},{11,9},{12,... | collective-permute-start | bytes 49160 | tf_op jit(solution)/shard_map/ppermute | solution.py:380
  62.2 33.5 %collective-permute-start.1 = (f32[4096]{0:T(1024)}, f32[4096]{0:T(1024)}, u32[]{:S(2)}, u32[]{:S(2)}) collective-permute-start(f32[4096]{0:T(1024)} %bitcast.22), channel_id=1, source_target_pairs={{1,0},{2,1},{3,2},{4,3},{5,4},{6,5},{7,6},{8,7},{9,8},{10,9},{11,1... | collective-permute-start | bytes 49160 | tf_op jit(solution)/shard_map/ppermute | solution.py:380
  64.3 31.4 %collective-permute-start.2 = (f32[4096]{0:T(1024)}, f32[4096]{0:T(1024)}, u32[]{:S(2)}, u32[]{:S(2)}) collective-permute-start(f32[4096]{0:T(1024)} %bitcast.22), channel_id=1, source_target_pairs={{0,1},{1,2},{2,3},{3,4},{4,5},{5,6},{6,7},{7,8},{8,9},{9,10},{10,1... | collective-permute-start | bytes 49160 | tf_op jit(solution)/shard_map/ppermute | solution.py:380
  71.4 24.3 %collective-permute-start.3 = (f32[4096]{0:T(1024)}, f32[4096]{0:T(1024)}, u32[]{:S(2)}, u32[]{:S(2)}) collective-permute-start(f32[4096]{0:T(1024)} %bitcast.22), channel_id=1, source_target_pairs={{0,2},{1,3},{2,4},{3,5},{4,6},{5,7},{6,8},{7,9},{8,10},{9,11},{10,... | collective-permute-start | bytes 49160 | tf_op jit(solution)/shard_map/ppermute | solution.py:380
  76.3 4.2 %copy-start.8 = (f32[12,4,4096]{2,1,0:T(4,128)}, f32[12,4,4096]{2,1,0:T(4,128)S(1)}, u32[]{:S(2)}) copy-start(f32[12,4,4096]{2,1,0:T(4,128)S(1)} %reshape.488) | copy-start | bytes 2359300
  80.5 3.2 %copy-start.3 = (f32[12,12,4096]{2,1,0:T(8,128)}, f32[12,12,4096]{2,1,0:T(8,128)S(1)}, u32[]{:S(2)}) copy-start(f32[12,12,4096]{2,1,0:T(8,128)S(1)} %pad_maximum_fusion) | copy-start | bytes 7077892
  81.5 3.1 %copy-start.1 = (bf16[8,224,384]{2,1,0:T(8,128)(2,1)S(1)}, bf16[8,224,384]{2,1,0:T(8,128)(2,1)}, u32[]{:S(2)}) copy-start(bf16[8,224,384]{2,1,0:T(8,128)(2,1)} %copy-done) | copy-start | bytes 4128772
  84.5 10.2 %copy-start.14 = (f32[12,4096]{1,0:T(8,128)S(1)}, f32[12,4096]{1,0:T(8,128)}, u32[]{:S(2)}) copy-start(f32[12,4096]{1,0:T(8,128)} %get-tuple-element.14) | copy-start | bytes 589828
  84.5 10.3 %copy-start.13 = (f32[12,4096]{1,0:T(8,128)S(1)}, f32[12,4096]{1,0:T(8,128)}, u32[]{:S(2)}) copy-start(f32[12,4096]{1,0:T(8,128)} %get-tuple-element.13) | copy-start | bytes 589828
  84.5 10.5 %copy-start.4 = (f32[12,12,4096]{2,1,0:T(8,128)S(1)}, f32[12,12,4096]{2,1,0:T(8,128)}, u32[]{:S(2)}) copy-start(f32[12,12,4096]{2,1,0:T(8,128)} %copy-done.3) | copy-start | bytes 7077892
  96.7 1.1 %copy-start.7 = (f32[12,4,4096]{2,1,0:T(4,128)S(1)}, f32[12,4,4096]{2,1,0:T(4,128)}, u32[]{:S(2)}) copy-start(f32[12,4,4096]{2,1,0:T(4,128)} %copy-done.5) | copy-start | bytes 2359300
  96.7 1.4 %copy-start.9 = (f32[12,4,4096]{2,1,0:T(4,128)S(1)}, f32[12,4,4096]{2,1,0:T(4,128)}, u32[]{:S(2)}) copy-start(f32[12,4,4096]{2,1,0:T(4,128)} %copy-done.8) | copy-start | bytes 2359300
  96.7 1.6 %copy-start.10 = (f32[12,4,4096]{2,1,0:T(4,128)S(1)}, f32[12,4,4096]{2,1,0:T(4,128)}, u32[]{:S(2)}) copy-start(f32[12,4,4096]{2,1,0:T(4,128)} %reshape.489) | copy-start | bytes 2359300
  98.3 0.9 copy-start.15
  101.4 0.9 copy-start.18
  101.4 1.0 copy-start.19
  103.5 1.0 copy-start.17
  (2 other events, 1.8 us)

commit v4 on v3

--- a/solution.py
+++ b/solution.py
@@ -307,6 +307,51 @@
     return out
 
 
+REACH = (-2, -1, 1, 2)
+
+
+def flux_kernel(sizes, row_ref, out_ref, send_sem, recv_sem):
+    sec_count, lat_count, col_count = sizes
+    devices = sec_count * lat_count * col_count
+    sec, lat, col = (lax.axis_index(name) for name in LINE)
+    line = (sec * lat_count + lat) * col_count + col
+    places = [place_of((line + devices - step) % devices, lat_count, col_count) for step in REACH]
+    barrier = pltpu.get_barrier_semaphore()
+    for place in places:
+        pl.semaphore_signal(barrier, inc=1, device_id=place, device_id_type=MESH)
+    pl.semaphore_wait(barrier, len(REACH))
+    copies = [
+        pltpu.make_async_remote_copy(
+            src_ref=row_ref,
+            dst_ref=out_ref.at[k],
+            send_sem=send_sem.at[k],
+            recv_sem=recv_sem.at[k],
+            device_id=place,
+            device_id_type=MESH,
+        )
+        for k, place in enumerate(places)
+    ]
+    for copy in copies:
+        copy.start()
+    for copy in copies:
+        copy.wait()
+
+
+def near_rows(sizes, row):
+    shape = (8, row.shape[0] // 8)
+    out = pl.pallas_call(
+        functools.partial(flux_kernel, sizes),
+        out_shape=jax.ShapeDtypeStruct((len(REACH),) + shape, row.dtype),
+        in_specs=[pl.BlockSpec(memory_space=pltpu.VMEM)],
+        out_specs=pl.BlockSpec(memory_space=pltpu.VMEM),
+        scratch_shapes=[pltpu.SemaphoreType.DMA((len(REACH),))] * 2,
+        compiler_params=pltpu.CompilerParams(
+            vmem_limit_bytes=2**20, collective_id=1, has_side_effects=True
+        ),
+    )(row.reshape(shape))
+    return out.reshape(len(REACH), row.shape[0])
+
+
 def legendre_kernel(degree_ref, slots_ref, weight_ref, coef_ref, out_ref):
     groups, lines, pair, width = coef_ref.shape
     rows = groups * lines
@@ -375,11 +420,6 @@
     return jnp.where(lane[None], spread, 0.0).sum(axis=1)
 
 
-def shifted(array, axis, count, step):
-    pairs = [(i, i + step) for i in range(count) if 0 <= i + step < count]
-    return lax.ppermute(array, axis, pairs)
-
-
 def advance_coupled_model(
     bordered_array,
     meridian_exchange_factor,
@@ -482,9 +522,8 @@
     speed_hi, speed_lo = split_two(speed)
     picked = pick_points([speed_hi, speed_lo, physical_state[0, 2 * strata + bottom]], column)
     flux = (picked[0] + picked[1]) * (mapped[0] + mapped[1] - picked[2])
-    flux_near = {
-        step: shifted(flux, LINE, devices, -step) if step else flux for step in (-2, -1, 0, 1, 2)
-    }
+    near = near_rows((lax.axis_size("sec"), lat_count, lax.axis_size("col")), flux)
+    flux_near = {0: flux, **{step: near[k] for k, step in enumerate(REACH)}}
 
     whole = jnp.concatenate([before, payload, after], axis=1)
     thermal = whole[:layers]

time: 108 us -> 95.5 us (0.88)
  the two profiles are of different devices: /device:TPU:27 before, /device:TPU:0 now
where the time goes in v4:
time: 95.5 us; the launch traced here: 94.8 us
  Pallas kernels  55.3 us (58%)
  local copies, waits for them, and re-layouts  21.1 us (22%)
  other arithmetic  13.4 us (14%)
  between operations  2.75 us (3%)
  matrix products  2.12 us (2%)
    pallas_call x1, Pallas kernels, exchange(): pl.pallas_call(functools.partial(exchange_kernel, sizes), out_shape=[jax....  37.6 us
    pallas_call x1, Pallas kernels, legendre(): pl.pallas_call(legendre_kernel, grid=(padded // SLOT_PAD,), out_shape=jax...  10.2 us
    unnamed x35, local copies, waits for them, and re-layouts  8.77 us
    pallas_call x1, Pallas kernels, near_rows(): pl.pallas_call(functools.partial(flux_kernel, sizes), out_shape=jax.Shape...  7.55 us
    add x4, other arithmetic, advance_coupled_model(): return centre + meridional + zonal_div + vertical + forced  4.27 us
    reshape x1, local copies, waits for them, and re-layouts, body(): after = after.reshape(payload.shape)  2.23 us
    dot_general x2, matrix products, pick_points(): jnp.einsum('kta,tx->kax', matrix, chosen, preferred_element_type=jnp.floa...  2.12 us

profile of v4, /device:TPU:0, one launch (start us, length us, event | category | flops | bytes accessed | tf_op | source)
XLA Modules:
  0.0 94.8 jit_solution(4759474989079382854)
XLA Ops:
  3.0 1.1 %constant_dynamic-update-slice_fusion = f32[12,4,4096]{2,1,0:T(4,128)S(1)} fusion(f32[8,4,4096]{2,1,0:T(4,128)} %param.14), kind=kLoop, calls=%fused_computation.163 | loop fusion | bytes 1048576
  4.3 0.9 copy-done.4
  5.9 2.6 %copy.13 = bf16[214,640,4]{0,1,2:T(8,128)(2,1)S(1)} copy(bf16[214,640,4]{1,2,0:T(4,128)(2,1)} %param.13) | data formatting | bytes 2191360 | tf_op args[3]
  8.5 1.2 %copy.14 = bf16[8,214,4,80]{1,3,2,0:T(8,128)(2,1)} copy(bf16[8,214,4,80]{1,3,0,2:T(8,128)(2,1)S(1)} %bitcast.102) | data formatting | bytes 2191360 | tf_op jit(solution)/shard_map/transpose | solution.py:488
  9.7 1.8 %copy.15 = bf16[8,214,320]{2,1,0:T(8,128)(2,1)S(1)} copy(bf16[8,214,320]{1,2,0:T(8,128)(2,1)} %bitcast.101) | data formatting | bytes 2191360 | tf_op jit(solution)/shard_map/reshape | solution.py:488
  11.6 0.9 copy-done.2
  12.5 37.6 %shard_map.113 = (bf16[8,4,224,128]{3,2,1,0:T(8,128)(2,1)S(1)}, bf16[8,224,384]{2,1,0:T(8,128)(2,1)S(1)}, bf16[48,4096]{1,0:T(8,128)(2,1)S(1)}, bf16[48,4096]{1,0:T(8,128)(2,1)S(1)}) custom-call(s32[1]{0:T(128)} %copy.25.points_ref, f32[2,60,640]{2,1,0:T(8,128)S(1)} %maximum_multiply_fusion.table_ref, s32[896,1]{1,0:T(8,128)S(1)} %reshape.506.slots_ref, ...), custom_call_target="tpu_custom_call" | custom-call | flops 838860800 | bytes 8388608 | tf_op jit(solution)/shard_map/pallas_call | solution.py:274
  50.2 1.1 %copy-done = bf16[8,224,384]{2,1,0:T(8,128)(2,1)} copy-done((bf16[8,224,384]{2,1,0:T(8,128)(2,1)}, bf16[8,224,384]{2,1,0:T(8,128)(2,1)S(1)}, u32[]{:S(2)}) %copy-start) | copy-done | bytes 1376280
  51.3 0.7 copy-done.3
  52.0 1.1 %select_convert_fusion = (f32[48,4096]{1,0:T(8,128)S(1)}, f32[48,4096]{1,0:T(8,128)S(1)}) fusion(bf16[48,4096]{1,0:T(8,128)(2,1)} %copy-done.3, pred[]{:T(512)S(6)} %eq.108, bf16[48,4096]{1,0:T(8,128)(2,1)S(1)} %get-tuple-element.8, pred[]{:T(512)S(6)} %eq.107), kind=kLoop, calls=%fused_computation.69 | loop fusion | flops 786432 | bytes 2359298 | tf_op jit(solution)/shard_map/convert_element_type | solution.py:504
  53.1 0.9 copy-done.8
  54.7 0.8 slice_bitcast_fusion.16
  56.2 0.9 fusion.11
  57.5 1.0 %sqrt_multiply_fusion = f32[1,1,5120]{2,1,0:T(1,128)S(1)} fusion(bf16[1,64,5120]{2,1,0:T(8,128)(2,1)} %param.10), kind=kLoop, calls=%fused_computation.136 | loop fusion | flops 35840 | bytes 40960 | tf_op jit(solution)/shard_map/mul | solution.py:519
  58.5 1.0 %slice_reduce_fusion = bf16[5120]{0:T(1024)(128)(2,1)S(1)} fusion(bf16[1,64,5120]{2,1,0:T(8,128)(2,1)} %param.10), kind=kLoop, calls=%fused_computation.137 | loop fusion | bytes 20480 | tf_op jit(solution)/shard_map/slice | solution.py:523
  59.5 1.2 %select_reduce_fusion = f32[3,4096]{1,0:T(4,128)S(1)} fusion(pred[128,4096]{1,0:T(8,128)(4,1)S(1)} %iota_compare_fusion.1, s32[4096]{0:T(1024)S(1)} %get-tuple-element.37, bf16[1,40,128]{2,1,0:T(8,128)(2,1)S(1)} %bitcast.110, bf16[1,40,128]{2,1,0:T(8,128)(2,1)S(1)} %get-tuple-element.30, bf16[1,40,128]{2,1,0:T(8,128)(2,1)S(1)} %get-tuple-element.29), kind=kOutput, calls=%fused_computation | convolution fusion | flops 129157120 | bytes 620544 | tf_op jit(solution)/shard_map/kta,tx->kax/dot_general | solution.py:418
  61.2 0.7 fusion.77
  62.0 7.5 %shard_map.115 = f32[4,8,512]{2,1,0:T(8,128)S(1)} custom-call(f32[8,512]{1,0:T(8,128)S(1)} %mul.393.row_ref), custom_call_target="tpu_custom_call" | custom-call | tf_op jit(solution)/shard_map/pallas_call | solution.py:342
  69.6 1.4 %reshape.499 = f32[12,4,4096]{2,1,0:T(4,128)S(1)} reshape(f32[48,4096]{1,0:T(8,128)} %copy-done.8) | data formatting | bytes 1572864 | tf_op jit(solution)/shard_map/reshape | solution.py:505
  70.9 2.2 %reshape.500 = f32[12,4,4096]{2,1,0:T(4,128)} reshape(f32[48,4096]{1,0:T(8,128)} %copy-done.7) | data formatting | bytes 1572864 | tf_op jit(solution)/shard_map/reshape | solution.py:506
  73.2 1.7 %pad_maximum_fusion = f32[12,12,4096]{2,1,0:T(8,128)S(1)} fusion(f32[12,4,4096]{2,1,0:T(4,128)} %reshape.500, f32[12,4,4096]{2,1,0:T(4,128)S(1)} %copy-done.5, f32[12,4,4096]{2,1,0:T(4,128)S(1)} %reshape.499), kind=kLoop, calls=%fused_computation.2 | loop fusion | flops 1179648 | bytes 4718592 | tf_op jit(solution)/shard_map/concatenate | solution.py:528
  77.5 1.7 %fusion.8 = f32[8,10,4096]{2,1,0:T(8,128)S(1)} fusion(f32[12,12,4096]{2,1,0:T(8,128)S(1)} %pad_maximum_fusion, f32[8,10,4096]{2,1,0:T(8,128)S(1)} %fusion.2, f32[8,10,4095]{2,1,0:T(8,128)S(1)} %bitcast.97, f32[8,10,1]{2,1,0:T(8,128)S(1)} %slice.442, f32[1,10,4096]{2,1,0:T(8,128)S(1)} %slice_bitcast_fusion, f32[7,10,4096]{2,1,0:T(8,128)S(1)} %fusion.10, ...), kind=kLoop, calls=%fused_computation.14 | loop fusion | flops 3932160 | bytes 9502720 | tf_op jit(solution)/shard_map/add | solution.py:442
  83.1 1.4 %fusion.37 = f32[8,4,4096]{2,1,0:T(4,128)} fusion(f32[8,6,4096]{2,1,0:T(8,128)S(1)} %fusion.17, f32[8,4,4096]{2,1,0:T(4,128)S(1)} %fusion.39, f32[8,4,4095]{2,1,0:T(4,128)S(1)} %bitcast.103, f32[8,4,1]{2,1,0:T(4,128)S(1)} %slice.493, f32[1,4,4096]{2,1,0:T(4,128)S(1)} %slice_bitcast_fusion.13, f32[7,4,4096]{2,1,0:T(4,128)S(1)} %fusion.42, ...), kind=kLoop, calls=%fused_computation.59 | loop fusion | flops 1572864 | bytes 3801088 | tf_op jit(solution)/shard_map/add | solution.py:442
  84.6 10.2 %shard_map.114 = f32[214,80,128]{2,1,0:T(8,128)} custom-call(s32[1]{0:T(128)} %bitcast.degree_ref, s32[224]{0:T(256)S(1)} %dynamic_slice.3.slots_ref, bf16[8,224,384]{2,1,0:T(8,128)(2,1)S(1)} %copy-done.1, bf16[8,4,224,128]{3,2,1,0:T(8,128)(2,1)S(1)} %get-tuple-element.7.coef_ref), custom_call_target="tpu_custom_call" | custom-call | flops 1174405120 | bytes 12435456 | tf_op jit(solution)/shard_map/pallas_call | solution.py:388
  (103 shorter events, 10.5 us)
Async XLA Ops:
  0.6 3.5 %copy-start.9 = (f32[4,4096]{1,0:T(4,128)S(1)}, f32[4,4096]{1,0:T(4,128)}, u32[]{:S(2)}) copy-start(f32[4,4096]{1,0:T(4,128)} %param.15) | copy-start | bytes 196612
  0.6 3.5 %copy-start.10 = (f32[4,4096]{1,0:T(4,128)S(1)}, f32[4,4096]{1,0:T(4,128)}, u32[]{:S(2)}) copy-start(f32[4,4096]{1,0:T(4,128)} %param.16) | copy-start | bytes 196612
  0.7 3.5 %copy-start.11 = (s32[4,4096]{1,0:T(4,128)S(1)}, s32[4,4096]{1,0:T(4,128)}, u32[]{:S(2)}) copy-start(s32[4,4096]{1,0:T(4,128)} %param.17) | copy-start | bytes 196612
  2.2 3.3 %copy-start.12 = (s32[856]{0:T(1024)S(1)}, s32[856]{0:T(1024)}, u32[]{:S(2)}) copy-start(s32[856]{0:T(1024)} %param.12) | copy-start | bytes 10276
  4.3 0.9 copy-start.4
  11.5 1.1 %copy-start.2 = (bf16[1,64,5120]{2,1,0:T(8,128)(2,1)S(1)}, bf16[1,64,5120]{2,1,0:T(8,128)(2,1)}, u32[]{:S(2)}) copy-start(bf16[1,64,5120]{2,1,0:T(8,128)(2,1)} %param.10) | copy-start | bytes 1966084
  50.2 1.1 %copy-start = (bf16[8,224,384]{2,1,0:T(8,128)(2,1)}, bf16[8,224,384]{2,1,0:T(8,128)(2,1)S(1)}, u32[]{:S(2)}) copy-start(bf16[8,224,384]{2,1,0:T(8,128)(2,1)S(1)} %get-tuple-element.6.weight_ref) | copy-start | bytes 4128772
  51.3 0.7 copy-start.3
  53.1 0.9 copy-start.8
  53.1 4.0 %copy-start.7 = (f32[48,4096]{1,0:T(8,128)}, f32[48,4096]{1,0:T(8,128)S(1)}, u32[]{:S(2)}) copy-start(f32[48,4096]{1,0:T(8,128)S(1)} %get-tuple-element.39) | copy-start | bytes 2359300
  60.7 12.5 %copy-start.5 = (f32[12,4,4096]{2,1,0:T(4,128)S(1)}, f32[12,4,4096]{2,1,0:T(4,128)}, u32[]{:S(2)}) copy-start(f32[12,4,4096]{2,1,0:T(4,128)} %copy-done.4) | copy-start | bytes 2359300
  75.8 1.1 %copy-start.6 = (f32[12,4,4096]{2,1,0:T(4,128)S(1)}, f32[12,4,4096]{2,1,0:T(4,128)}, u32[]{:S(2)}) copy-start(f32[12,4,4096]{2,1,0:T(4,128)} %reshape.500) | copy-start | bytes 2359300
  83.1 1.6 %copy-start.1 = (bf16[8,224,384]{2,1,0:T(8,128)(2,1)S(1)}, bf16[8,224,384]{2,1,0:T(8,128)(2,1)}, u32[]{:S(2)}) copy-start(bf16[8,224,384]{2,1,0:T(8,128)(2,1)} %copy-done) | copy-start | bytes 4128772
